TPU v7x, 32 devices: a whole 2x2x4 slice. The times are simulated.
32 devices in a mesh: dp: 4 (over z), chan: 2 (over y), hid: 4 (over x, core).
Axes of the slice: x: 2, y: 2, z: 4, core: 2. Of those that a mesh axis runs over, the one named last changes fastest.
Arguments:
- patches: bfloat16 [96, 196, 768], P(('dp', 'hid'), None, 'chan'), may hold values from -6 to 6
- cotangent: bfloat16 [96, 196, 768], P(('dp', 'hid'), None, 'chan'), may hold values from -6 to 6
- live_images: int32 [16], P(('dp', 'hid')), may hold values from 3 to 6, as said below
- first_gain: bfloat16 [768], P('chan'), may hold values from 0.099609375 to 1.8984375
- first_shift: bfloat16 [768], P('chan'), may hold values from -2 to 2
- token_up: bfloat16 [196, 384], replicated, may hold values from -0.4375 to 0.4375
- token_up_bias: bfloat16 [384], replicated, may hold values from -3 to 3
- token_down: bfloat16 [384, 196], replicated, may hold values from -0.3125 to 0.3125
- token_down_bias: bfloat16 [196], replicated, may hold values from -2 to 2
- second_gain: bfloat16 [768], P('chan'), may hold values from 0.099609375 to 1.8984375
- second_shift: bfloat16 [768], P('chan'), may hold values from -2 to 2
- chan_up: bfloat16 [768, 3072], P(None, 'hid'), may hold values from -0.21875 to 0.21875
- chan_up_bias: bfloat16 [3072], P('hid'), may hold values from -3 to 3
- chan_down: bfloat16 [3072, 768], P('hid', 'chan'), may hold values from -0.109375 to 0.109375
- chan_down_bias: bfloat16 [768], P('chan'), may hold values from -2 to 2
Outputs:
- mixed: bfloat16 [96, 196, 768], P(('dp', 'hid'), None, 'chan')
- input_grad: bfloat16 [96, 196, 768], P(('dp', 'hid'), None, 'chan')
- grad_first_gain: float32 [768], P('chan')
- grad_first_shift: float32 [768], P('chan')
- grad_token_up: float32 [196, 384], replicated
- grad_token_up_bias: float32 [384], replicated
- grad_token_down: float32 [384, 196], replicated
- grad_token_down_bias: float32 [196], replicated
- grad_second_gain: float32 [768], P('chan')
- grad_second_shift: float32 [768], P('chan')
- grad_chan_up: float32 [768, 3072], P(None, 'hid')
- grad_chan_up_bias: float32 [3072], P('hid')
- grad_chan_down: float32 [3072, 768], P('hid', 'chan')
- grad_chan_down_bias: float32 [768], P('chan')
Inputs may be any that keep to these rules, and one draw needn't show every extreme that they name: Each group holds live_images[g] real images in its first slots, the rest are padding; some group is full and some holds exactly 3 images.
All inputs are finite; a program needn't handle non-finite values.
Results may differ from a plain program's by a relative error of at most 0.0065.
Values may be sent and summed in bfloat16 or wider, within the bound.
A program may use at most 192 MiB of HBM per device.

v0:
```python
import jax
import jax.numpy as jnp
from jax import lax
from jax.sharding import PartitionSpec as P

EPS = 1e-06


def normalize(values, sums, width):
    mean = sums[0][..., None] / width
    spread = sums[1][..., None] / width - mean * mean
    inv_std = lax.rsqrt(spread + EPS)
    return ((values - mean) * inv_std, inv_std)


def along_rows(left, right):
    return lax.dot_general(
        left, right, (((0,), (0,)), ((), ())), preferred_element_type=jnp.float32
    )


def against_cols(left, right):
    return lax.dot_general(
        left, right, (((1,), (1,)), ((), ())), preferred_element_type=jnp.float32
    )


def body(
    patches,
    cotangent,
    live_images,
    first_gain,
    first_shift,
    token_up,
    token_up_bias,
    token_down,
    token_down_bias,
    second_gain,
    second_shift,
    chan_up,
    chan_up_bias,
    chan_down,
    chan_down_bias,
):
    images, patch_count, local_width = patches.shape
    width = local_width * lax.axis_size("chan")
    rows = images * patch_count
    keep = (jnp.arange(images, dtype=jnp.int32) < live_images[0]).astype(jnp.float32)[:, None, None]
    inputs = patches.astype(jnp.float32)
    first_sums = lax.psum((jnp.sum(inputs, -1), jnp.sum(inputs * inputs, -1)), "chan")
    normed_one, inv_one = normalize(inputs, first_sums, width)
    token_in = (
        normed_one * first_gain.astype(jnp.float32) + first_shift.astype(jnp.float32)
    ).astype(jnp.bfloat16)
    token_pre = (
        jnp.einsum("bpc,pk->bkc", token_in, token_up, preferred_element_type=jnp.float32)
        + token_up_bias.astype(jnp.float32)[None, :, None]
    )
    token_act, token_back = jax.vjp(jax.nn.gelu, token_pre)
    token_hidden = token_act.astype(jnp.bfloat16)
    mixed_once = (
        inputs
        + jnp.einsum("bkc,kp->bpc", token_hidden, token_down, preferred_element_type=jnp.float32)
        + token_down_bias.astype(jnp.float32)[None, :, None]
    )
    second_sums = lax.psum((jnp.sum(mixed_once, -1), jnp.sum(mixed_once * mixed_once, -1)), "chan")
    normed_two, inv_two = normalize(mixed_once, second_sums, width)
    chan_in = (
        (normed_two * second_gain.astype(jnp.float32) + second_shift.astype(jnp.float32))
        .astype(jnp.bfloat16)
        .reshape(rows, local_width)
    )
    chan_cols = lax.all_gather(chan_in, "chan", axis=1, tiled=True)
    chan_rows = lax.all_gather(chan_cols, "hid", axis=0, tiled=True)
    chan_pre = jnp.dot(
        chan_rows, chan_up, preferred_element_type=jnp.float32
    ) + chan_up_bias.astype(jnp.float32)
    chan_act, chan_back = jax.vjp(jax.nn.gelu, chan_pre)
    chan_hidden = chan_act.astype(jnp.bfloat16)
    branch = lax.psum_scatter(
        jnp.dot(chan_hidden, chan_down, preferred_element_type=jnp.float32),
        "hid",
        scatter_dimension=0,
        tiled=True,
    )
    branch = (branch + chan_down_bias.astype(jnp.float32)).reshape(images, patch_count, local_width)
    result = keep * (mixed_once + branch)
    out_back = keep * cotangent.astype(jnp.float32)
    out_low = out_back.reshape(rows, local_width).astype(jnp.bfloat16)
    grad_down_bias = jnp.sum(out_low.astype(jnp.float32), 0)
    grad_cols, down_cols = (
        lax.all_gather(out_low, "chan", axis=1, tiled=True),
        lax.all_gather(chan_down, "chan", axis=1, tiled=True),
    )
    chan_slot = lax.axis_index("chan") * local_width
    grad_rows = lax.all_gather(grad_cols, "hid", axis=0, tiled=True)
    hidden_grad = against_cols(grad_rows, down_cols)
    pre_grad = chan_back(hidden_grad)[0].astype(jnp.bfloat16)
    grad_up = along_rows(chan_rows, pre_grad)
    grad_up_bias = jnp.sum(pre_grad.astype(jnp.float32), 0)
    grad_down = along_rows(
        chan_hidden, lax.dynamic_slice_in_dim(grad_rows, chan_slot, local_width, 1)
    )
    up_mine = lax.dynamic_slice_in_dim(chan_up, chan_slot, local_width, 0)
    normed_grad = lax.psum_scatter(
        against_cols(pre_grad, up_mine), "hid", scatter_dimension=0, tiled=True
    )
    grad_up, grad_up_bias, grad_down = lax.psum((grad_up, grad_up_bias, grad_down), "dp")
    normed_grad = normed_grad.reshape(images, patch_count, local_width)
    grad_second_gain = jnp.sum(normed_grad * normed_two, (0, 1))
    grad_second_shift = jnp.sum(normed_grad, (0, 1))
    scaled_two = normed_grad * second_gain.astype(jnp.float32)
    back_sums = lax.psum((jnp.sum(scaled_two, -1), jnp.sum(scaled_two * normed_two, -1)), "chan")
    residual_grad = out_back + inv_two * (
        scaled_two - back_sums[0][..., None] / width - normed_two * back_sums[1][..., None] / width
    )
    branch_low = residual_grad.astype(jnp.bfloat16)
    grad_token_down_bias = jnp.sum(branch_low.astype(jnp.float32), (0, 2))
    grad_token_down = jnp.einsum(
        "bkc,bpc->kp", token_hidden, branch_low, preferred_element_type=jnp.float32
    )
    token_grad = jnp.einsum(
        "bpc,kp->bkc", branch_low, token_down, preferred_element_type=jnp.float32
    )
    token_pre_grad = token_back(token_grad)[0].astype(jnp.bfloat16)
    grad_token_up_bias = jnp.sum(token_pre_grad.astype(jnp.float32), (0, 2))
    grad_token_up = jnp.einsum(
        "bpc,bkc->pk", token_in, token_pre_grad, preferred_element_type=jnp.float32
    )
    first_grad = jnp.einsum(
        "bkc,pk->bpc", token_pre_grad, token_up, preferred_element_type=jnp.float32
    )
    grad_first_gain = jnp.sum(first_grad * normed_one, (0, 1))
    grad_first_shift = jnp.sum(first_grad, (0, 1))
    scaled_one = first_grad * first_gain.astype(jnp.float32)
    (
        sum_plain,
        sum_cross,
        grad_token_up,
        grad_token_up_bias,
        grad_token_down,
        grad_token_down_bias,
    ) = lax.psum(
        (
            jnp.sum(scaled_one, -1),
            jnp.sum(scaled_one * normed_one, -1),
            grad_token_up,
            grad_token_up_bias,
            grad_token_down,
            grad_token_down_bias,
        ),
        "chan",
    )
    input_grad = residual_grad + inv_one * (
        scaled_one - sum_plain[..., None] / width - normed_one * sum_cross[..., None] / width
    )
    totals = lax.psum(
        (
            grad_token_up,
            grad_token_up_bias,
            grad_token_down,
            grad_token_down_bias,
            grad_first_gain,
            grad_first_shift,
            grad_second_gain,
            grad_second_shift,
            grad_down_bias,
        ),
        ("dp", "hid"),
    )
    return (
        result.astype(jnp.bfloat16),
        input_grad.astype(jnp.bfloat16),
        totals[4],
        totals[5],
        totals[0],
        totals[1],
        totals[2],
        totals[3],
        totals[6],
        totals[7],
        grad_up,
        grad_up_bias,
        grad_down,
        totals[8],
    )


def solution(mesh):
    in_specs = (
        P(("dp", "hid"), None, "chan"),
        P(("dp", "hid"), None, "chan"),
        P(("dp", "hid")),
        P("chan"),
        P("chan"),
        P(),
        P(),
        P(),
        P(),
        P("chan"),
        P("chan"),
        P(None, "hid"),
        P("hid"),
        P("hid", "chan"),
        P("chan"),
    )
    out_specs = (
        P(("dp", "hid"), None, "chan"),
        P(("dp", "hid"), None, "chan"),
        P("chan"),
        P("chan"),
        P(),
        P(),
        P(),
        P(),
        P("chan"),
        P("chan"),
        P(None, "hid"),
        P("hid"),
        P("hid", "chan"),
        P("chan"),
    )
    return jax.shard_map(body, mesh=mesh, in_specs=in_specs, out_specs=out_specs, check_vma=False)
```

profile of v0, /device:TPU:0, one launch (start us, length us, event | category | flops | bytes accessed | tf_op | source)
XLA Modules:
  0.0 693.8 jit_solution(5883137355580422990)
XLA Ops:
  13.1 9.6 %all-reduce.8 = (f32[6,196]{1,0:T(8,128)S(1)}, f32[6,196]{1,0:T(8,128)S(1)}) all-reduce(f32[6,196]{1,0:T(8,128)S(1)} %get-tuple-element.24, f32[6,196]{1,0:T(8,128)S(1)} %get-tuple-element.23), channel_id=1, replica_groups=mesh['dp'=4,'chan'=2,'hid'=4] {'chan'}, use_global_device_ids=true, to_apply=%region_3.0 | all-reduce | flops 2352 | bytes 18816 | tf_op jit(solution)/shard_map/psum | solution.py:50
  27.4 6.7 all-reduce.7
  43.0 26.2 %all-gather.6.cloned.1.call-done = bf16[1176,768]{1,0:T(8,128)(2,1)} async-done(((bf16[1176,384]{1,0:T(8,128)(2,1)}), bf16[1176,768]{1,0:T(8,128)(2,1)}) %all-gather.6.cloned.1.call-update) | async-done | bytes 1806352 | tf_op jit(solution)/shard_map/all_gather | solution.py:73
  69.8 31.3 %all-gather.10.cloned.1.call-done = bf16[1176,768]{1,0:T(8,128)(2,1)} async-done(((bf16[1176,384]{1,0:T(8,128)(2,1)}), bf16[1176,768]{1,0:T(8,128)(2,1)}) %all-gather.10.cloned.1.call-update) | async-done | bytes 1806352 | tf_op jit(solution)/shard_map/all_gather | solution.py:92
  101.4 53.0 %all-gather.8.cloned.1.call-done = bf16[4704,768]{1,0:T(8,128)(2,1)} async-done(((bf16[1176,768]{1,0:T(8,128)(2,1)}), bf16[4704,768]{1,0:T(8,128)(2,1)}) %all-gather.8.cloned.1.call-update) | async-done | bytes 7225360 | tf_op jit(solution)/shard_map/all_gather | solution.py:74
  154.5 11.7 %fusion.58 = f32[4704,768]{1,0:T(8,128)} fusion(bf16[4704,768]{1,0:T(8,128)(2,1)} %all-gather.8.cloned.1.call-done, bf16[768,768]{1,0:T(8,128)(2,1)S(1)} %copy-done), kind=kOutput, calls=%fused_computation.88 | convolution fusion | flops 5549064192 | bytes 22855680 | tf_op jit(solution)/shard_map/dot_general | solution.py:75
  166.2 12.5 %all-gather.14.cloned.1.call-done = bf16[768,768]{1,0:T(8,128)(2,1)} async-done(((bf16[768,384]{1,0:T(8,128)(2,1)}), bf16[768,768]{1,0:T(8,128)(2,1)}) %all-gather.14.cloned.1.call-update) | async-done | bytes 1179664 | tf_op jit(solution)/shard_map/all_gather | solution.py:93
  178.7 53.1 %all-gather.12.cloned.1.call-done = bf16[4704,768]{1,0:T(8,128)(2,1)} async-done(((bf16[1176,768]{1,0:T(8,128)(2,1)}), bf16[4704,768]{1,0:T(8,128)(2,1)}) %all-gather.12.cloned.1.call-update) | async-done | bytes 7225360 | tf_op jit(solution)/shard_map/all_gather | solution.py:96
  231.8 19.9 %convert_reduce_fusion = (f32[768]{0:T(1024)S(1)}, bf16[4704,768]{1,0:T(8,128)(2,1)}, bf16[4704,768]{1,0:T(8,128)(2,1)S(1)}) fusion(f32[4704,768]{1,0:T(8,128)} %fusion.58, f32[768]{0:T(1024)S(1)} %convert_element_type.97, bf16[4704,768]{1,0:T(8,128)(2,1)} %all-gather.12.cloned.1.call-done, bf16[768,768]{1,0:T(8,128)(2,1)} %all-gather.14.cloned.1.call-done), kind=kOutput, calls=%fused_computation.9 | convolution fusion | flops 5639379968 | bytes 37312512 | tf_op jit(solution)/shard_map/dot_general | solution.py:23
  254.7 5.9 fusion.59
  260.6 8.7 %fusion.38 = f32[4704,384]{1,0:T(8,128)} fusion(bf16[4704,768]{1,0:T(8,128)(2,1)} %get-tuple-element.49, bf16[768,768]{1,0:T(8,128)(2,1)S(1)} %copy-done, s32[]{:T(128)S(6)} %select_n.4), kind=kOutput, calls=%fused_computation.67 | convolution fusion | flops 2774532096 | bytes 15040516 | tf_op jit(solution)/shard_map/dot_general | solution.py:23
  270.1 12.7 %fusion.60 = f32[768,768]{1,0:T(8,128)} fusion(bf16[4704,768]{1,0:T(8,128)(2,1)} %all-gather.8.cloned.1.call-done, bf16[4704,768]{1,0:T(8,128)(2,1)} %get-tuple-element.49), kind=kOutput, calls=%fused_computation.90 | convolution fusion | flops 5549064192 | bytes 16809984 | tf_op jit(solution)/shard_map/dot_general | solution.py:17
  282.8 42.6 %reduce-scatter.7.cloned.1.call-done = f32[1176,384]{1,0:T(8,128)} async-done(((f32[4704,384]{1,0:T(8,128)}), f32[1176,384]{1,0:T(8,128)}) %reduce-scatter.7.cloned.1.call-update) | async-done | bytes 1806352
  330.9 61.9 %reduce-scatter.9.cloned.1.call-done = f32[1176,384]{1,0:T(8,128)} async-done(((f32[4704,384]{1,0:T(8,128)}), f32[1176,384]{1,0:T(8,128)}) %reduce-scatter.9.cloned.1.call-update) | async-done | bytes 1806352
  398.3 8.1 %all-reduce.6 = (f32[6,196]{1,0:T(8,128)S(1)}, f32[6,196]{1,0:T(8,128)S(1)}) all-reduce(f32[6,196]{1,0:T(8,128)S(1)} %get-tuple-element.15, f32[6,196]{1,0:T(8,128)S(1)} %reduce_sum.151), channel_id=1, replica_groups=mesh['dp'=4,'chan'=2,'hid'=4] {'chan'}, use_global_device_ids=true, to_apply=%region_13.0 | all-reduce | flops 2352 | bytes 18816 | tf_op jit(solution)/shard_map/psum | solution.py:113
  406.4 3.8 convert_reduce_fusion.4
  418.4 9.1 %fusion.7 = f32[768,384]{1,0:T(8,128)} fusion(bf16[4704,768]{1,0:T(8,128)(2,1)} %copy-done.13, bf16[4704,768]{1,0:T(8,128)(2,1)} %all-gather.12.cloned.1.call-done, s32[]{:T(128)S(6)} %select_n.4), kind=kOutput, calls=%fused_computation.13 | convolution fusion | flops 2774532096 | bytes 12017668 | tf_op jit(solution)/shard_map/dot_general | solution.py:17
  427.5 12.5 %psum.189 = f32[768]{0:T(1024)} all-reduce(f32[768]{0:T(1024)S(1)} %get-tuple-element.48), channel_id=1, replica_groups=mesh['dp'=4,'chan'=2,'hid'=4] {'dp'}, use_global_device_ids=true, to_apply=%region_38.0 | all-reduce | flops 768 | bytes 6144 | tf_op jit(solution)/shard_map/psum | solution.py:108
  440.1 3.8 fusion.33
  445.6 7.3 %all-reduce.5 = (f32[6,196]{1,0:T(8,128)S(1)}, f32[6,196]{1,0:T(8,128)S(1)}, f32[384]{0:T(512)S(1)}, f32[196]{0:T(256)S(1)}) all-reduce(f32[6,196]{1,0:T(8,128)S(1)} %get-tuple-element.17, f32[6,196]{1,0:T(8,128)S(1)} %get-tuple-element.18, f32[384]{0:T(512)S(1)} %get-tuple-element.62, ...), channel_id=1, replica_groups=mesh['dp'=4,'chan'=2,'hid'=4] {'chan'}, use_global_device_ids=true, to_apply=%region_17.0 | all-reduce | flops 2932 | bytes 23456 | tf_op jit(solution)/shard_map/psum | solution.py:143
  453.0 61.9 %all-reduce.2 = (f32[384]{0:T(512)}, f32[384]{0:T(512)}, f32[384]{0:T(512)}, f32[196]{0:T(256)}, f32[384]{0:T(512)}, /*index=5*/f32[384]{0:T(512)}, f32[384]{0:T(512)}) all-reduce(f32[384]{0:T(512)S(1)} %get-tuple-element.16, f32[384]{0:T(512)S(1)} %reduce_sum.156, ...), channel_id=1, replica_groups=mesh['dp'=4,'chan'=2,'hid'=4] {'dp','hid'}, use_global_device_ids=true, to_apply=%region_19.0 | all-reduce | flops 2500 | bytes 20000 | tf_op jit(solution)/shard_map/psum | solution.py:157
  518.1 68.4 %all-reduce.16.cloned.1.call-done = (f32[768,768]{1,0:T(8,128)}, f32[768,384]{1,0:T(8,128)}) async-done(((f32[768,768]{1,0:T(8,128)}, f32[768,384]{1,0:T(8,128)}), (f32[768,768]{1,0:T(8,128)}, f32[768,384]{1,0:T(8,128)})) %all-reduce.16.cloned.1.call-update) | async-done | bytes 3538960 | tf_op jit(solution)/shard_map/psum | solution.py:108
  586.4 92.8 %all-reduce.14.cloned.1.call-done = (f32[196,384]{1,0:T(8,128)}, f32[384,196]{0,1:T(8,128)}) async-done(((f32[196,384]{1,0:T(8,128)}, f32[384,196]{0,1:T(8,128)}), (f32[196,384]{1,0:T(8,128)}, f32[384,196]{0,1:T(8,128)})) %all-reduce.14.cloned.1.call-update) | async-done | bytes 602128 | tf_op jit(solution)/shard_map/psum | solution.py:157
  682.7 3.3 copy.50
  (85 shorter events, 51.9 us)
Async XLA Ops:
  7.2 147.3 %copy-start = (bf16[768,768]{1,0:T(8,128)(2,1)S(1)}, bf16[768,768]{1,0:T(8,128)(2,1)}, u32[]{:S(2)}) copy-start(bf16[768,768]{1,0:T(8,128)(2,1)} %param.26) | copy-start | bytes 3538948
  7.2 62.0 %all-gather.6.cloned.1.call-start = ((), (), s32[]{:S(2)}) async-start(), calls=%async_computation.2 | async-start | bytes 2709504 | tf_op jit(solution)/shard_map/all_gather | solution.py:73
  22.7 2.7 copy-start.1
  22.7 2.7 copy-start.12
  25.4 2.0 copy-start.5
  37.6 63.6 %all-gather.10.cloned.1.call-start = ((), (), s32[]{:S(2)}) async-start(), calls=%async_computation.4 | async-start | bytes 2709504 | tf_op jit(solution)/shard_map/all_gather | solution.py:92
  43.0 111.5 %all-gather.8.cloned.1.call-start = ((), (), s32[]{:S(2)}) async-start(), calls=%async_computation.3 | async-start | bytes 9031680 | tf_op jit(solution)/shard_map/all_gather | solution.py:74
  69.2 32.2 %copy-start.10 = (bf16[768]{0:T(1024)(128)(2,1)S(1)}, bf16[768]{0:T(1024)(128)(2,1)}, u32[]{:S(2)}) copy-start(bf16[768]{0:T(1024)(128)(2,1)} %param.27) | copy-start | bytes 4612
  69.2 109.5 %all-gather.14.cloned.1.call-start = ((), (), s32[]{:S(2)}) async-start(), calls=%async_computation.6 | async-start | bytes 1769472 | tf_op jit(solution)/shard_map/all_gather | solution.py:93
  69.8 162.0 %all-gather.12.cloned.1.call-start = ((), (), s32[]{:S(2)}) async-start(), calls=%async_computation.5 | async-start | bytes 9031680 | tf_op jit(solution)/shard_map/all_gather | solution.py:96
  101.2 224.2 %reduce-scatter.7.cloned.1.call-start = ((), (), s32[]{:S(2)}) async-start(), calls=%async_computation.7 | async-start | bytes 9031680
  231.8 22.9 %copy-start.8 = (bf16[768,384]{1,0:T(8,128)(2,1)S(1)}, bf16[768,384]{1,0:T(8,128)(2,1)}, u32[]{:S(2)}) copy-start(bf16[768,384]{1,0:T(8,128)(2,1)} %param.28) | copy-start | bytes 1769476
  251.7 3.0 copy-start.13
  260.6 132.3 %reduce-scatter.9.cloned.1.call-start = ((), (), s32[]{:S(2)}) async-start(), calls=%async_computation.8 | async-start | bytes 9031680
  269.4 245.4 %all-reduce.18.cloned.1.call-start = ((), (), s32[]{:S(2)}) async-start(), calls=%async_computation.11 | async-start | bytes 1228800 | tf_op jit(solution)/shard_map/psum | solution.py:143
  395.6 2.4 copy-start.4
  406.4 3.8 copy-start.6
  410.2 2.3 copy-start.3
  412.5 4.3 copy-start.2
  415.6 1.2 copy-start.14
  418.3 168.1 %all-reduce.16.cloned.1.call-start = ((), (), s32[]{:S(2)}) async-start(), calls=%async_computation.10 | async-start | bytes 7077888 | tf_op jit(solution)/shard_map/psum | solution.py:108
  427.5 12.6 %copy-start.9 = (bf16[196,384]{1,0:T(8,128)(2,1)S(1)}, bf16[196,384]{1,0:T(8,128)(2,1)}, u32[]{:S(2)}) copy-start(bf16[196,384]{1,0:T(8,128)(2,1)} %param.20) | copy-start | bytes 451588
  427.5 251.8 %all-reduce.14.cloned.1.call-start = ((), (), s32[]{:S(2)}) async-start(), calls=%async_computation.9 | async-start | bytes 1228800 | tf_op jit(solution)/shard_map/psum | solution.py:157
  682.7 3.3 copy-start.7
  (1 other events, 0.7 us)
Sparse Core Ops, SparseCore 0:
  37.7 31.3 all-gather.5
  71.3 29.8 all-gather.9
  102.7 51.6 all-gather.7
  155.9 22.7 all-gather.13
  180.1 51.6 all-gather.11
  260.7 64.6 reduce-scatter.6
  328.1 64.7 reduce-scatter.8
  418.4 30.1 all-reduce.17
  451.6 134.7 all-reduce.15
  589.7 89.4 all-reduce.13
where the time goes:
time: 695 us; the launch traced here: 694 us
  waiting for transfers between devices  443 us (64%)
  blocking collectives  106 us (15%)
  matrix products  83.4 us (12%)
  other arithmetic  23.9 us (3%)
  local copies, waits for them, and re-layouts  22.1 us (3%)
  between operations  15 us (2%)
    unnamed x12, waiting for transfers between devices  105 us
    psum x1, waiting for transfers between devices, body(): lax.psum((grad_token_up, grad_token_up_bias, grad_token_down, grad_token_...  92.8 us
    psum x1, waiting for transfers between devices, body(): lax.psum((grad_up, grad_up_bias, grad_down), 'dp')  68.4 us
    psum x1, blocking collectives, body(): lax.psum((grad_token_up, grad_token_up_bias, grad_token_down, grad_token_...  61.9 us
    all_gather x1, waiting for transfers between devices, body(): grad_rows = lax.all_gather(grad_cols, 'hid', axis=0, tiled=True)  53.1 us
    all_gather x1, waiting for transfers between devices, body(): chan_rows = lax.all_gather(chan_cols, 'hid', axis=0, tiled=True)  53 us
    all_gather x1, waiting for transfers between devices, body(): lax.all_gather(out_low, 'chan', axis=1, tiled=True)  31.3 us
    dot_general x2, matrix products, against_cols(): lax.dot_general(left, right, (((1,), (1,)), ((), ())), preferred_element_...  28.6 us
  transfers between devices with their start and end apart: 10, of which 9 were waited for; matrix products, arithmetic and copies ran while one was open for 9% of the time, Pallas kernels for 0%

commit v1 on v0

v1 whole, which is shorter than its diff:
```python
import functools

import jax
import jax.numpy as jnp
from jax import lax
from jax.experimental import pallas as pl
from jax.experimental.pallas import tpu as pltpu
from jax.sharding import PartitionSpec as P

EPS = 1e-06
BF = jnp.bfloat16
F32 = jnp.float32
MESH = pl.DeviceIdType.MESH
TANH_A = 0.7978845608028654
TANH_B = TANH_A * 0.044715


def nn(left, right):
    return lax.dot_general(left, right, (((1,), (0,)), ((), ())), preferred_element_type=F32)


def nt(left, right):
    return lax.dot_general(left, right, (((1,), (1,)), ((), ())), preferred_element_type=F32)


def tn(left, right):
    return lax.dot_general(left, right, (((0,), (0,)), ((), ())), preferred_element_type=F32)


def gelu_pair(v):
    square = v * v
    tanh = jnp.tanh(v * (TANH_A + TANH_B * square))
    half = 0.5 + 0.5 * tanh
    value = v * half
    slope = half + value * (1.0 - tanh) * (TANH_A + 3.0 * TANH_B * square)
    return value, slope


def pad_rows(count):
    return -(-count // 16) * 16


class Sizes:
    def __init__(self, mesh_shape, patches, chan_up, token_up):
        self.dp = mesh_shape["dp"]
        self.chan = mesh_shape["chan"]
        self.hid = mesh_shape["hid"]
        self.xs = self.hid // 2
        self.images, self.s, self.l = patches
        self.ps = pad_rows(self.s + 1)
        self.d = 2 * self.l
        self.own = self.images // 2
        self.f = chan_up[1]
        self.ds = token_up[1]
        self.chunks = self.f // self.l
        self.plane = self.chan * self.hid
        groups = 3 + self.hid * self.chunks
        unit = 16 * self.plane
        self.vec_row = 2 * self.ps
        self.small = -(-(self.vec_row + 8 * groups) // unit) * unit
        self.groups = (self.small - self.vec_row) // 8
        self.piece = self.small // self.plane
        self.levels = self.dp.bit_length() - 1
        self.seg = 2 * self.l // self.dp
        assert self.chan == 2 and self.hid % 2 == 0 and self.images % 2 == 0
        assert 1 << self.levels == self.dp and self.f % self.l == 0 and self.ds == self.l


def kernel(
    o,
    live_ref, patches_ref, cot_ref, ut_ref, up_ref, dn_ref, dt_ref, tdb_ref, vec_ref, bias_ref, chan_up_ref, chan_down_ref,
    mixed_out, grad_out, gup_out, gdn_out, small_out,
    pat, cot, cot_in, stats, stats_in, means, tin, th, tslope, msend, mrecv, rows_m, rows_n, inv2, vec_in,
    xs_all, gs_all, w_up, w_dn, w_b, hid_s, pg_s, out_acc, ng_acc, xch_send, ng_in, out_in,
    blow, bl_send, mo_send, scaled, gacc, vecs,
    gb, rx, ry, tot, fin, rz, small_send, small_in, small_z,
    loc_sem, send_sem, recv_sem,
):
    z = lax.axis_index("dp")
    y = lax.axis_index("chan")
    h = lax.axis_index("hid")
    c = h % 2
    x = h // 2
    S, PS, L, OWN, IM, F = o.s, o.ps, o.l, o.own, o.images, o.f
    width = float(o.d)

    def dev(zz=None, yy=None, xx=None, cc=None):
        zz = z if zz is None else zz
        yy = y if yy is None else yy
        xx = x if xx is None else xx
        cc = c if cc is None else cc
        return (zz, yy, xx * 2 + cc)

    partner = dev(yy=1 - y)
    sibling = dev(cc=1 - c)
    counter = [0]

    def take(count=1):
        base = counter[0]
        counter[0] += count
        return base

    def remote(src, dst, device, index=None):
        index = take() if index is None else index
        return pltpu.make_async_remote_copy(
            src_ref=src, dst_ref=dst, send_sem=send_sem.at[index], recv_sem=recv_sem.at[index],
            device_id=device, device_id_type=MESH,
        )

    loads = []

    def load(src, dst):
        copy = pltpu.make_async_copy(src, dst, loc_sem.at[len(loads)])
        loads.append(copy)
        copy.start()
        return copy

    load_pat = load(patches_ref, pat)
    load_cot = load(cot_ref, cot)
    load_up0 = load(chan_up_ref.at[pl.ds(pl.multiple_of(y * L, L), L)], w_up.at[0, pl.ds(0, L)])
    load_up1 = load(chan_up_ref.at[pl.ds(pl.multiple_of((1 - y) * L, L), L)], w_up.at[0, pl.ds(L, L)])
    load_dn = load(chan_down_ref, w_dn.at[0, :, pl.ds(0, L)])
    load_b = load(bias_ref, w_b.at[0])

    pad = PS - S
    pad_row = lax.broadcasted_iota(jnp.int32, (pad, L), 0)
    one_row = jnp.where(pad_row == 0, 1.0, 0.0).astype(BF)
    for j in range(IM):
        tin[j, S:PS, :] = one_row
    xs_all[...] = jnp.zeros(xs_all.shape, BF)
    gs_all[...] = jnp.zeros(gs_all.shape, BF)
    rows_n[...] = jnp.zeros(rows_n.shape, F32)
    rows_m[...] = jnp.zeros(rows_m.shape, F32)
    inv2[...] = jnp.zeros(inv2.shape, F32)
    stats[...] = jnp.zeros(stats.shape, F32)
    msend[...] = jnp.zeros(msend.shape, BF)
    mo_send[...] = jnp.zeros(mo_send.shape, BF)
    vecs[...] = jnp.zeros(vecs.shape, F32)
    gacc[...] = jnp.zeros(gacc.shape, F32)

    barrier = pltpu.get_barrier_semaphore()
    here = y * o.hid + h
    for step in range(1, o.plane):
        there = (here + step) % o.plane
        pl.semaphore_signal(barrier, inc=1, device_id=(z, there // o.hid, there % o.hid), device_id_type=MESH)
    for step in range(1, o.dp):
        pl.semaphore_signal(barrier, inc=1, device_id=((z + step) % o.dp, y, h), device_id_type=MESH)
    pl.semaphore_wait(barrier, o.plane - 1 + o.dp - 1)

    lane = lax.broadcasted_iota(jnp.int32, (S, 128), 1)
    load_pat.wait()

    def sums_of(j, acc):
        v = pat[j].astype(F32)
        acc = jnp.where(lane == j, jnp.sum(v, -1, keepdims=True), acc)
        return jnp.where(lane == j + 64, jnp.sum(v * v, -1, keepdims=True), acc)

    stats[0, :S, :] = lax.fori_loop(0, IM, sums_of, jnp.zeros((S, 128), F32))
    copy_stats = remote(stats.at[0], stats_in.at[0], partner)
    copy_stats.start()
    copy_vec = remote(vec_ref, vec_in, partner)
    copy_vec.start()

    copy_dn = [None] * o.xs
    copy_dn2 = [None] * o.xs
    copy_up = [None] * o.xs
    copy_up2 = [None] * o.xs
    copy_b = [None] * o.xs
    mine_rows = pl.ds(pl.multiple_of(y * L, L), L)
    other_rows = pl.ds(pl.multiple_of((1 - y) * L, L), L)
    copy_dn2[0] = remote(chan_down_ref, w_dn.at[0, :, pl.ds(L, L)], partner)
    copy_dn2[0].start()
    copy_cot = remote(cot_ref.at[pl.ds((1 - y) * OWN, OWN)], cot_in, partner)
    copy_cot.start()
    for step in range(1, o.xs):
        there = (x + step) % o.xs
        copy_b[step] = remote(bias_ref, w_b.at[step], dev(xx=there))
        copy_up[step] = remote(chan_up_ref.at[mine_rows], w_up.at[step, pl.ds(0, L)], dev(xx=there))
        copy_up2[step] = remote(chan_up_ref.at[other_rows], w_up.at[step, pl.ds(L, L)], dev(xx=there))
        copy_dn[step] = remote(chan_down_ref, w_dn.at[step, :, pl.ds(0, L)], dev(xx=there))
        copy_dn2[step] = remote(chan_down_ref, w_dn.at[step, :, pl.ds(L, L)], dev(xx=there, yy=1 - y))
        for copy in (copy_b, copy_up, copy_up2, copy_dn, copy_dn2):
            copy[step].start()

    copy_stats.wait()
    total = (stats[0] + stats_in[0]) * (1.0 / width)
    inv = lax.rsqrt(pltpu.roll(total, 64, 1) - total * total + EPS)
    wide_lane = lax.broadcasted_iota(jnp.int32, (PS, 128), 1)
    means[...] = jnp.where(wide_lane < 64, total, pltpu.roll(inv, 64, 1))

    def column(ref_rows, j):
        return jnp.sum(jnp.where(lane == j, ref_rows, 0.0), -1, keepdims=True)

    first_gain = vec_ref[0:1, :]
    first_shift = vec_ref[1:2, :]

    def first_norm(j):
        table = means[:S, :]
        inv_one = column(table, j + 64)
        return (pat[j].astype(F32) - column(table, j)) * inv_one, inv_one

    def token_forward(j):
        normed, _ = first_norm(j)
        tin[j, :S, :] = (normed * first_gain + first_shift).astype(BF)
        value, slope = gelu_pair(nn(ut_ref[...], tin[j]))
        th[j] = value.astype(BF)
        tslope[j] = slope.astype(BF)
        back = nn(dt_ref[...], th[j])
        return pat[j].astype(F32) + back[:S] + tdb_ref[:S, :]

    mixed_sems = take(OWN)

    def copy_mixed(i):
        return remote(msend.at[i], mrecv.at[i], partner, mixed_sems + i)

    @pl.loop(0, OWN)
    def _(i):
        msend[i, :S, :] = token_forward((1 - y) * OWN + i).astype(BF)
        copy_mixed(i).start()

    @pl.loop(0, OWN)
    def _(i):
        rows_m[i, :S, :L] = token_forward(y * OWN + i)

    load_cot.wait()
    copy_cot.wait()
    live = live_ref[0]

    def keep_of(j):
        return jnp.where(j < live, 1.0, 0.0).astype(F32)

    @pl.loop(0, OWN)
    def _(i):
        keep = keep_of(y * OWN + i)
        gs_all[c, i, :S, :L] = (cot[y * OWN + i].astype(F32) * keep).astype(BF)
        gs_all[c, i, :S, L:] = (cot_in[i].astype(F32) * keep).astype(BF)

    copy_gs = remote(gs_all.at[c], gs_all.at[c], sibling)
    copy_gs.start()

    copy_vec.wait()
    both = [jnp.concatenate([vec_ref[k:k + 1, :], vec_in[k:k + 1, :]], axis=1) for k in range(2, 5)]
    second_gain, second_shift, down_bias = both
    row_sems = take(OWN)

    def copy_rows(i):
        return remote(xs_all.at[c, i], xs_all.at[c, i], sibling, row_sems + i)

    @pl.loop(0, OWN)
    def _(i):
        copy_mixed(i).wait()
        rows_m[i, :S, L:] = mrecv[i, :S, :].astype(F32)
        v = rows_m[i, :S, :]
        mean = jnp.sum(v, -1, keepdims=True) * (1.0 / width)
        spread = jnp.sum(v * v, -1, keepdims=True) * (1.0 / width) - mean * mean
        inv_two = lax.rsqrt(spread + EPS)
        normed = (v - mean) * inv_two
        inv2[i, :S, :] = inv_two
        rows_n[i, :S, :] = normed
        xs_all[c, i, :S, :] = (normed * second_gain + second_shift).astype(BF)
        copy_rows(i).start()

    rows = OWN * PS
    load_up0.wait()
    load_up1.wait()
    load_dn.wait()
    load_b.wait()
    copy_gs.wait()

    @pl.loop(0, OWN)
    def _(i):
        copy_rows(i).wait()

    order = [0] + list(range(1, o.xs))
    copy_gx = {}
    first = True
    for step in order:
        if step:
            copy_b[step].wait()
            copy_up[step].wait()
            copy_up2[step].wait()
            copy_dn[step].wait()
        copy_dn2[step].wait()
        for part in range(o.chunks):
            cols = pl.ds(part * L, L)

            def side(cc, total, first=first, step=step, cols=cols):
                xin = xs_all[cc].reshape(rows, o.d)
                gin = gs_all[cc].reshape(rows, o.d)
                value, slope = gelu_pair(nn(xin, w_up[step, :, cols]) + w_b[step, 0:1, cols])
                hidden = value.astype(BF)
                hid_s[cc] = hidden
                down = w_dn[step, cols, :]
                add_out = nn(hidden, down)
                pre = (nt(gin, down) * slope).astype(BF)
                pg_s[cc] = pre
                add_ng = nt(pre, w_up[step, :, cols])
                if first:
                    out_acc[cc] = add_out
                    ng_acc[cc] = add_ng
                else:
                    out_acc[cc] += add_out
                    ng_acc[cc] += add_ng
                return total + jnp.sum(pre.astype(F32), 0, keepdims=True)

            up_bias_grad = lax.fori_loop(0, 2, side, jnp.zeros((1, L), F32))
            owner = ((x + o.xs - step) % o.xs * 2 + c) * o.chunks + part
            vecs[3 + owner, 0:1, :] = up_bias_grad
            first = False
            for half in range(2):
                lanes = pl.ds(half * L, L)
                xin = xs_all[:, :, :, lanes].reshape(2 * rows, L)
                gin = gs_all[:, :, :, lanes].reshape(2 * rows, L)
                gb[step, part, half, 0] = tn(xin, pg_s[...].reshape(2 * rows, L)).astype(BF)
                gb[step, part, half, 1] = tn(hid_s[...].reshape(2 * rows, L), gin).astype(BF)
            if step:
                copy = remote(gb.at[step, part], rx.at[step - 1, part], dev(xx=(x + o.xs - step) % o.xs))
                copy.start()
                copy_gx[step, part] = copy

    xch_send[0] = ng_acc[1 - c].astype(BF)
    copy_ng = remote(xch_send.at[0], ng_in, sibling)
    copy_ng.start()
    xch_send[1] = out_acc[1 - c].astype(BF)
    copy_out = remote(xch_send.at[1], out_in, sibling)
    copy_out.start()

    res_sems = take(OWN)

    def copy_res(i):
        return remote(bl_send.at[i], blow.at[y * OWN + i], partner, res_sems + i)

    copy_ng.wait()

    def residual(i, sums):
        block = pl.ds(pl.multiple_of(i * PS, 16), PS)
        ng = ng_acc[c, block, :] + ng_in[block, :].astype(F32)
        normed = rows_n[i]
        back = gs_all[c, i].astype(F32)
        sums = (
            sums[0] + jnp.sum(ng * normed, 0, keepdims=True),
            sums[1] + jnp.sum(ng, 0, keepdims=True),
            sums[2] + jnp.sum(back, 0, keepdims=True),
        )
        q = ng * second_gain
        m1 = jnp.sum(q, -1, keepdims=True) * (1.0 / width)
        m2 = jnp.sum(q * normed, -1, keepdims=True) * (1.0 / width)
        res = (back + inv2[i] * (q - m1 - normed * m2)).astype(BF)
        bl_send[i] = res[:, L:]
        copy_res(i).start()
        blow[y * OWN + i] = res[:, :L]
        return sums

    zero = jnp.zeros((1, o.d), F32)
    sums = lax.fori_loop(0, OWN, residual, (zero, zero, zero))
    for k in range(3):
        vecs[0, 1 + 2 * k:2 + 2 * k, :] = jnp.where(y == 0, sums[k][:, :L], sums[k][:, L:])
        vecs[0, 2 + 2 * k:3 + 2 * k, :] = jnp.where(y == 0, sums[k][:, L:], sums[k][:, :L])

    copy_out.wait()
    mixed_sems2 = take(OWN)

    def copy_mo(i):
        return remote(mo_send.at[i], mixed_out.at[y * OWN + i], partner, mixed_sems2 + i)

    @pl.loop(0, OWN)
    def _(i):
        block = pl.ds(pl.multiple_of(i * PS, 16), PS)
        branch = out_acc[c, block, :] + out_in[block, :].astype(F32) + down_bias
        result = (keep_of(y * OWN + i) * (rows_m[i] + branch)).astype(BF)
        mo_send[i] = result[:, L:]
        copy_mo(i).start()
        mixed_out[y * OWN + i] = result[:, :L]

    ones = jnp.ones((16, L), BF)

    def token_backward(j, carry):
        acc, sum_gain, sum_shift, sum_bias = carry
        low = blow[j]
        grad = (nn(dn_ref[...], low) * tslope[j].astype(F32)).astype(BF)
        gacc[0] += nt(tin[j], grad)
        gacc[1] += nt(low, th[j])
        sum_bias = sum_bias + nt(ones, low)
        back = nn(up_ref[...], grad)[:S]
        normed, _ = first_norm(j)
        sum_gain = sum_gain + jnp.sum(back * normed, 0, keepdims=True)
        sum_shift = sum_shift + jnp.sum(back, 0, keepdims=True)
        back = back * first_gain
        scaled[j, :S, :] = back
        acc = jnp.where(lane == j, jnp.sum(back, -1, keepdims=True), acc)
        acc = jnp.where(lane == j + 64, jnp.sum(back * normed, -1, keepdims=True), acc)
        return acc, sum_gain, sum_shift, sum_bias

    carry = (jnp.zeros((S, 128), F32), jnp.zeros((1, L), F32), jnp.zeros((1, L), F32), jnp.zeros((16, PS), F32))
    carry = lax.fori_loop(0, OWN, lambda i, t: token_backward(y * OWN + i, t), carry)

    def later(i, t):
        copy_res(i).wait()
        return token_backward((1 - y) * OWN + i, t)

    acc, sum_gain, sum_shift, sum_bias = lax.fori_loop(0, OWN, later, carry)
    stats[1, :S, :] = acc
    copy_stats2 = remote(stats.at[1], stats_in.at[1], partner)
    copy_stats2.start()
    vecs[0, 0:1, :PS] = sum_bias[0:1, :]
    vecs[1 + y, 0:1, :] = sum_gain
    vecs[1 + y, 1:2, :] = sum_shift

    def piece(k):
        return pl.ds(pl.multiple_of(k * o.piece, 16), o.piece)

    small_send[0:PS, :] = gacc[0].astype(BF)
    small_send[PS:2 * PS, :] = gacc[1].astype(BF)
    small_send[o.vec_row:, :] = vecs[...].reshape(8 * o.groups, L).astype(BF)
    copy_small = []
    for step in range(1, o.plane):
        there = (here + step) % o.plane
        copy = remote(small_send.at[piece(there)], small_in.at[step - 1], (z, there // o.hid, there % o.hid))
        copy.start()
        copy_small.append(copy)

    copy_stats2.wait()
    means2 = (stats[1, :S, :] + stats_in[1, :S, :]) * (1.0 / width)

    @pl.loop(0, IM)
    def _(j):
        normed, inv_one = first_norm(j)
        grad = scaled[j, :S, :] - column(means2, j) - normed * column(means2, j + 64)
        grad_out[j, :S, :] = (blow[j, :S, :].astype(F32) + inv_one * grad).astype(BF)
        grad_out[j, S:, :] = jnp.zeros((PS - S, L), BF)

    for copy in copy_small:
        copy.wait()
    mine = small_send[piece(here), :].astype(F32)
    for step in range(1, o.plane):
        mine = mine + small_in[step - 1].astype(F32)
    small_z[z] = mine.astype(BF)
    copy_z = []
    for step in range(1, o.dp):
        copy = remote(small_z.at[z], small_z.at[z], ((z + step) % o.dp, y, h))
        copy.start()
        copy_z.append(copy)

    copy_gy = []
    for part in range(o.chunks):
        for step in range(1, o.xs):
            copy_gx[step, part].wait()
        for half in range(2):
            for kind in range(2):
                mine = gb[0, part, half, kind].astype(F32)
                for step in range(1, o.xs):
                    mine = mine + rx[step - 1, part, half, kind].astype(F32)
                gb[0, part, half, kind] = mine.astype(BF)
        copy = remote(gb.at[0, part, 1], ry.at[part], partner)
        copy.start()
        copy_gy.append(copy)

    for copy in copy_z:
        copy.wait()
    mine = small_z[0].astype(F32)
    for k in range(1, o.dp):
        mine = mine + small_z[k].astype(F32)
    small_out[piece(here), :] = mine.astype(BF)
    copy_sf = []
    for step in range(1, o.plane):
        there = (here + step) % o.plane
        copy = remote(small_out.at[piece(here)], small_out.at[piece(here)], (z, there // o.hid, there % o.hid))
        copy.start()
        copy_sf.append(copy)

    half_seg = o.dp // 2
    for part in range(o.chunks):
        copy_gy[part].wait()
        for kind in range(2):
            mine = gb[0, part, 0, kind].astype(F32) + ry[part, kind].astype(F32)
            for k in range(half_seg):
                tot[part, kind * half_seg + k] = mine[k * o.seg:(k + 1) * o.seg].astype(BF)
    start, count, used = 0, o.dp, 0
    spans = []
    for level in range(o.levels):
        bit = (z // (1 << level)) % 2
        peer = dev(zz=z + (1 - 2 * bit) * (1 << level))
        count //= 2
        keep_at, send_at = start + bit * count, start + (1 - bit) * count
        copies = []
        for part in range(o.chunks):
            copy = remote(tot.at[part, pl.ds(send_at, count)], rz.at[part, pl.ds(used, count)], peer)
            copy.start()
            copies.append(copy)
        for part in range(o.chunks):
            copies[part].wait()
            mine = tot[part, pl.ds(keep_at, count)].astype(F32) + rz[part, pl.ds(used, count)].astype(F32)
            (fin if count == 1 else tot)[part, pl.ds(keep_at, count)] = mine.astype(BF)
        spans.append((keep_at, count, peer))
        start = keep_at
        used += count
    for keep_at, count, peer in reversed(spans):
        copies = []
        for part in range(o.chunks):
            span = fin.at[part, pl.ds(keep_at, count)]
            copy = remote(span, span, peer)
            copy.start()
            copies.append(copy)
        for copy in copies:
            copy.wait()
    copies = []
    for part in range(o.chunks):
        copy = remote(fin.at[part, pl.ds(0, half_seg)], gup_out.at[part, y], partner)
        copy.start()
        copies.append(copy)
        gup_out[part, y] = fin[part, :half_seg]
        gdn_out[part] = fin[part, half_seg:]

    @pl.loop(0, OWN)
    def _(i):
        copy_mo(i).wait()

    for copy in copies + copy_sf:
        copy.wait()


def block_call(o, live, patches, cot, ut, up, dn, dt, tdb, vec, bias, chan_up, chan_down):
    I, S, PS, L, OWN, D, X, C = o.images, o.s, o.ps, o.l, o.own, o.d, o.xs, o.chunks
    half_seg = o.dp // 2
    any_spec = pl.BlockSpec(memory_space=pl.ANY)
    vmem = pl.BlockSpec(memory_space=pltpu.VMEM)
    rows = OWN * PS
    copies = 2 + 1 + 1 + 5 * (X - 1) + 3 * OWN + 1 + (X - 1) * C + 2 + OWN + 1
    copies += 2 * (o.plane - 1) + o.dp - 1 + C + 2 * o.levels * C + C + 8
    outs = [
        jax.ShapeDtypeStruct((I, PS, L), BF),
        jax.ShapeDtypeStruct((I, PS, L), BF),
        jax.ShapeDtypeStruct((C, 2, half_seg, o.seg, L), BF),
        jax.ShapeDtypeStruct((C, half_seg, o.seg, L), BF),
        jax.ShapeDtypeStruct((o.small, L), BF),
    ]
    scratch = [
        ((I, S, L), BF), ((I, S, L), BF), ((OWN, S, L), BF),
        ((2, PS, 128), F32), ((2, PS, 128), F32), ((PS, 128), F32),
        ((I, PS, L), BF), ((I, o.ds, L), BF), ((I, o.ds, L), BF),
        ((OWN, PS, L), BF), ((OWN, PS, L), BF),
        ((OWN, PS, D), F32), ((OWN, PS, D), F32), ((OWN, PS, 1), F32), ((8, L), F32),
        ((2, OWN, PS, D), BF), ((2, OWN, PS, D), BF),
        ((X, D, o.f), BF), ((X, o.f, D), BF), ((X, 8, o.f), F32),
        ((2, rows, L), BF), ((2, rows, L), BF), ((2, rows, D), F32), ((2, rows, D), F32),
        ((2, rows, D), BF), ((rows, D), BF), ((rows, D), BF),
        ((I, PS, L), BF), ((OWN, PS, L), BF), ((OWN, PS, L), BF), ((I, PS, L), F32),
        ((2, PS, L), F32), ((o.groups, 8, L), F32),
        ((X, C, 2, 2, L, L), BF), ((X - 1, C, 2, 2, L, L), BF), ((C, 2, L, L), BF),
        ((C, o.dp, o.seg, L), BF), ((C, o.dp, o.seg, L), BF), ((C, o.dp - 1, o.seg, L), BF),
        ((o.small, L), BF), ((o.plane - 1, o.piece, L), BF), ((o.dp, o.piece, L), BF),
    ]
    return pl.pallas_call(
        functools.partial(kernel, o),
        out_shape=outs,
        in_specs=[pl.BlockSpec(memory_space=pltpu.SMEM), any_spec, any_spec] + [vmem] * 7 + [any_spec] * 2,
        out_specs=[vmem] * 5,
        scratch_shapes=[pltpu.VMEM(shape, kind) for shape, kind in scratch]
        + [pltpu.SemaphoreType.DMA((8,)), pltpu.SemaphoreType.DMA((copies,)), pltpu.SemaphoreType.DMA((copies,))],
        compiler_params=pltpu.CompilerParams(
            collective_id=1, has_side_effects=True, vmem_limit_bytes=63 * 2**20
        ),
        name="mixer_block",
    )(live, patches, cot, ut, up, dn, dt, tdb, vec, bias, chan_up, chan_down)


def body(
    o,
    patches,
    cotangent,
    live_images,
    first_gain,
    first_shift,
    token_up,
    token_up_bias,
    token_down,
    token_down_bias,
    second_gain,
    second_shift,
    chan_up,
    chan_up_bias,
    chan_down,
    chan_down_bias,
):
    S, PS, L = o.s, o.ps, o.l
    rest = PS - S
    up = jnp.pad(token_up, ((0, rest), (0, 0)))
    ut = jnp.concatenate([token_up, token_up_bias[None], jnp.zeros((rest - 1, o.ds), BF)], 0).T
    dn = jnp.pad(token_down, ((0, 0), (0, rest)))
    dt = jnp.pad(token_down.T, ((0, rest), (0, 0)))
    tdb = jnp.pad(token_down_bias.astype(F32), (0, rest))[:, None]
    vec = jnp.stack([first_gain, first_shift, second_gain, second_shift, chan_down_bias] + [jnp.zeros((L,), BF)] * 3)
    bias = jnp.broadcast_to(chan_up_bias.astype(F32)[None], (8, o.f))
    mixed, grad, gup, gdn, small = block_call(
        o, live_images, patches, cotangent, ut, up, dn, dt, tdb, vec.astype(F32), bias, chan_up, chan_down
    )
    y = lax.axis_index("chan")
    h = lax.axis_index("hid")
    small = small.astype(F32)
    groups = small[o.vec_row:].reshape(o.groups, 8, L)

    def pick(at, row):
        return lax.dynamic_slice_in_dim(groups[:, row], at, 1, 0)[0]

    def pick_half(row):
        return lax.dynamic_slice_in_dim(groups[0], row + y, 1, 0)[0]

    return (
        mixed[:, :S],
        grad[:, :S],
        pick(1 + y, 0),
        pick(1 + y, 1),
        small[:S],
        small[S],
        small[PS:PS + S].T,
        groups[0, 0, :S],
        pick_half(1),
        pick_half(3),
        gup.reshape(o.chunks, 2, L, L).transpose(1, 2, 0, 3).reshape(o.d, o.f).astype(F32),
        lax.dynamic_slice_in_dim(groups[:, 0], 3 + h * o.chunks, o.chunks, 0).reshape(o.f),
        gdn.reshape(o.f, L).astype(F32),
        pick_half(5),
    )


def solution(mesh):
    in_specs = (
        P(("dp", "hid"), None, "chan"),
        P(("dp", "hid"), None, "chan"),
        P(("dp", "hid")),
        P("chan"),
        P("chan"),
        P(),
        P(),
        P(),
        P(),
        P("chan"),
        P("chan"),
        P(None, "hid"),
        P("hid"),
        P("hid", "chan"),
        P("chan"),
    )
    out_specs = (
        P(("dp", "hid"), None, "chan"),
        P(("dp", "hid"), None, "chan"),
        P("chan"),
        P("chan"),
        P(),
        P(),
        P(),
        P(),
        P("chan"),
        P("chan"),
        P(None, "hid"),
        P("hid"),
        P("hid", "chan"),
        P("chan"),
    )

    def whole(*args):
        shape = dict(mesh.shape)
        patches, token_up, chan_up = args[0].shape, args[5].shape, args[11].shape
        local = (patches[0] // (shape["dp"] * shape["hid"]), patches[1], patches[2] // shape["chan"])
        o = Sizes(shape, local, (chan_up[0], chan_up[1] // shape["hid"]), token_up)
        mapped = jax.shard_map(
            functools.partial(body, o), mesh=mesh, in_specs=in_specs, out_specs=out_specs, check_vma=False
        )
        return mapped(*args)

    return whole
```

time: 695 us -> 249 us (0.36)
  waiting for transfers between devices: 443 us -> 0 us
  Pallas kernels: 0 us -> 227 us
  blocking collectives: 106 us -> 0 us
  matrix products: 83.4 us -> 0 us
  other arithmetic: 23.9 us -> 2.86 us
  between operations: 15 us -> 1.56 us
    pallas_call x0 -> x1, Pallas kernels: none -> 227 us  [block_call(): pl.pallas_call(functools.partial(kernel, o), out_shape=outs, in_specs=[pl...]
    all_gather x5 -> x0, waiting for transfers between devices: 176 us -> none  [the longest x1 53.1 us: body(): grad_rows = lax.all_gather(grad_cols, 'hid', axis=0, tiled=True)]
    psum x3 -> x0, waiting for transfers between devices: 161 us -> none  [the longest x1 92.8 us: body(): lax.psum((grad_token_up, grad_token_up_bias, grad_token_down, grad_token_...]
    psum x6 -> x0, blocking collectives: 106 us -> none  [the longest x1 61.9 us: body(): lax.psum((grad_token_up, grad_token_up_bias, grad_token_down, grad_token_...]
    unnamed x12 -> x0, waiting for transfers between devices: 105 us -> none
    dot_general x12 -> x0, matrix products: 83.4 us -> none  [the longest x2 28.6 us: against_cols(): lax.dot_general(left, right, (((1,), (1,)), ((), ())), preferred_element_...]
    reduce_sum x6 -> x0, other arithmetic: 12.4 us -> none  [the longest x1 3.76 us: body(): grad_token_down_bias = jnp.sum(branch_low.astype(jnp.float32), (0, 2))]
    unnamed x34 -> x27, local copies, waits for them, and re-layouts: 12.4 us -> 2.83 us
  transfers between devices with their start and end apart: 10 -> 0, of which waited for: 9 -> 0; matrix products, arithmetic and copies ran while one was open for 9% -> 0% of each run, Pallas kernels for 0% -> 0%
where the time goes in v1:
time: 249 us
  Pallas kernels  227 us (91%)
  local copies, waits for them, and re-layouts  17.2 us (7%)
  other arithmetic  2.86 us (1%)
    pallas_call x1, Pallas kernels, block_call(): pl.pallas_call(functools.partial(kernel, o), out_shape=outs, in_specs=[pl...  227 us

profile of v1, /device:TPU:0, one launch (start us, length us, event | category | flops | bytes accessed | tf_op | source)
XLA Modules:
  0.0 249.0 jit_solution(14209639919711624614)
XLA Ops:
  1.3 0.8 broadcast_in_dim.23
  2.2 1.1 copy.32
  3.3 0.1 pad.22.clone
  3.4 0.8 maximum_bitcast_fusion.ut_ref
  4.2 1.6 pad.16.up_ref
  5.8 0.1 copy.34
  5.9 0.7 pad.17.dn_ref
  6.6 0.7 pad.18.dt_ref
  7.3 0.8 copy.35.tdb_ref
  8.2 0.6 convert_element_type.35.vec_ref
  8.8 0.6 broadcast_in_dim.21.bias_ref
  9.5 227.3 %mixer_block.1 = (bf16[6,208,384]{2,1,0:T(8,128)(2,1)}, bf16[6,208,384]{2,1,0:T(8,128)(2,1)}, bf16[2,2,2,192,384]{4,3,2,1,0:T(8,128)(2,1)}, bf16[2,2,192,384]{3,2,1,0:T(8,128)(2,1)}, bf16[512,384]{1,0:T(8,128)(2,1)}) custom-call(s32[1]{0:T(128)S(6)} %copy.38.live_ref, bf16[6,196,384]{2,1,0:T(8,128)(2,1)} %patches_ref.1, bf16[6,196,384]{2,1,0:T(8,128)(2,1)} %cot_ref.1, ...), custom_call_target="tpu_custom_call" | custom-call | tf_op jit(solution)/shard_map/mixer_block/pallas_call | solution.py:553
  236.8 2.3 slice.35
  239.1 1.0 slice.36
  240.2 0.6 dynamic-slice_reduce_fusion.4
  240.8 0.7 slice.48
  241.6 0.6 dynamic-slice_reduce_fusion.1
  242.2 0.7 slice_bitcast_fusion
  242.9 0.6 slice.51
  243.5 0.3 convert_bitcast_fusion
  243.8 1.8 copy.36
  245.6 1.6 copy.37
  247.2 0.6 reshape.55
  247.8 1.1 bitcast_convert_fusion
  (39 shorter events, 0.3 us)
Async XLA Ops:
  0.6 5.1 %copy-start.3 = (bf16[384,196]{0,1:T(8,128)(2,1)S(1)}, bf16[384,196]{0,1:T(8,128)(2,1)}, u32[]{:S(2)}) copy-start(bf16[384,196]{0,1:T(8,128)(2,1)} %param.22) | copy-start | bytes 451588
  0.7 6.6 %copy-start.11 = (bf16[196]{0:T(256)(128)(2,1)S(1)}, bf16[196]{0:T(256)(128)(2,1)}, u32[]{:S(2)}) copy-start(bf16[196]{0:T(256)(128)(2,1)} %param.23) | copy-start | bytes 1180
  2.1 5.9 %copy-start.6 = (bf16[384]{0:T(512)(128)(2,1)S(1)}, bf16[384]{0:T(512)(128)(2,1)}, u32[]{:S(2)}) copy-start(bf16[384]{0:T(512)(128)(2,1)} %param.18) | copy-start | bytes 2308
  2.2 5.9 %copy-start.7 = (bf16[384]{0:T(512)(128)(2,1)S(1)}, bf16[384]{0:T(512)(128)(2,1)}, u32[]{:S(2)}) copy-start(bf16[384]{0:T(512)(128)(2,1)} %param.19) | copy-start | bytes 2308
  2.2 5.9 %copy-start.8 = (bf16[384]{0:T(512)(128)(2,1)S(1)}, bf16[384]{0:T(512)(128)(2,1)}, u32[]{:S(2)}) copy-start(bf16[384]{0:T(512)(128)(2,1)} %param.24) | copy-start | bytes 2308
  2.2 5.9 %copy-start.9 = (bf16[384]{0:T(512)(128)(2,1)S(1)}, bf16[384]{0:T(512)(128)(2,1)}, u32[]{:S(2)}) copy-start(bf16[384]{0:T(512)(128)(2,1)} %param.25) | copy-start | bytes 2308
  2.2 6.0 %copy-start.10 = (bf16[384]{0:T(512)(128)(2,1)S(1)}, bf16[384]{0:T(512)(128)(2,1)}, u32[]{:S(2)}) copy-start(bf16[384]{0:T(512)(128)(2,1)} %param.29) | copy-start | bytes 2308
  2.2 6.6 %copy-start.5 = (bf16[768]{0:T(1024)(128)(2,1)S(1)}, bf16[768]{0:T(1024)(128)(2,1)}, u32[]{:S(2)}) copy-start(bf16[768]{0:T(1024)(128)(2,1)} %param.27) | copy-start | bytes 4612
  236.8 2.3 copy-start.2
  239.1 1.0 copy-start
  240.1 3.4 %copy-start.1 = (bf16[2,2,2,192,384]{4,3,2,1,0:T(8,128)(2,1)S(1)}, bf16[2,2,2,192,384]{4,3,2,1,0:T(8,128)(2,1)}, u32[]{:S(2)}) copy-start(bf16[2,2,2,192,384]{4,3,2,1,0:T(8,128)(2,1)} %get-tuple-element.22) | copy-start | bytes 3538948
  245.6 2.2 copy-start.4

commit v2 on v1

v2 whole, which is shorter than its diff:
```python
import functools

import jax
import jax.numpy as jnp
from jax import lax
from jax.experimental import pallas as pl
from jax.experimental.pallas import tpu as pltpu
from jax.sharding import PartitionSpec as P

EPS = 1e-06
BF = jnp.bfloat16
F32 = jnp.float32
MESH = pl.DeviceIdType.MESH
TANH_A = 0.7978845608028654
TANH_B = TANH_A * 0.044715


def nn(left, right):
    return lax.dot_general(left, right, (((1,), (0,)), ((), ())), preferred_element_type=F32)


def nt(left, right):
    return lax.dot_general(left, right, (((1,), (1,)), ((), ())), preferred_element_type=F32)


def tn(left, right):
    return lax.dot_general(left, right, (((0,), (0,)), ((), ())), preferred_element_type=F32)


def gelu_pair(v):
    square = v * v
    tanh = jnp.tanh(v * (TANH_A + TANH_B * square))
    half = 0.5 + 0.5 * tanh
    value = v * half
    slope = half + value * (1.0 - tanh) * (TANH_A + 3.0 * TANH_B * square)
    return value, slope


def pad_rows(count):
    return -(-count // 16) * 16


class Sizes:
    ways = (("xyz", "yxz"), ("zxy", "yxz"))
    plan = {
        ("M", 0, "grad"): ((0, 1),),
        ("O", 1, "side"): ((0, 0),),
        ("M", 1, "side"): ((0, 0), (0, 1), (1, 0)),
        ("M", 1, "grad"): ((1, 1), (1, 0)),
        ("residual",): ((0, 0), (0, 1)),
        ("token own",): ((1, 0),),
        ("token other",): ((0, 0), (0, 1), (1, 0), (1, 1)),
        ("norm",): ((0, 0), (0, 1), (1, 0), (1, 1)),
        ("end",): ("small", (0, 0), (0, 1), (1, 0), (1, 1)),
    }

    def __init__(self, mesh_shape, patches, chan_up, token_up):
        self.dp = mesh_shape["dp"]
        self.chan = mesh_shape["chan"]
        self.hid = mesh_shape["hid"]
        self.xs = self.hid // 2
        self.images, self.s, self.l = patches
        self.ps = pad_rows(self.s + 1)
        self.d = 2 * self.l
        self.own = self.images // 2
        self.f = chan_up[1]
        self.ds = token_up[1]
        self.chunks = self.f // self.l
        self.plane = self.chan * self.hid
        units = [(part, kind) for part in range(self.chunks) for kind in range(2)]
        self.firsts = [(part, kind) for part, kind in units if self.ways[part % 2][kind] == "zxy"]
        self.slots = [(part, kind, half) for part, kind in units for half in range(1 + ((part, kind) in self.firsts))]
        groups = 3 + self.hid * self.chunks
        unit = 16 * self.plane
        self.vec_row = 2 * self.ps
        self.small = -(-(self.vec_row + 8 * groups) // unit) * unit
        self.groups = (self.small - self.vec_row) // 8
        self.piece = self.small // self.plane
        self.levels = self.dp.bit_length() - 1
        self.seg = self.l // self.dp
        self.wide = -(-self.ps // 128) * 128
        assert self.images <= 8
        assert self.chan == 2 and self.hid % 2 == 0 and self.images % 2 == 0
        assert 1 << self.levels == self.dp and self.f % self.l == 0 and self.ds == self.l


def kernel(
    o,
    live_ref, patches_ref, cot_ref, ut_ref, up_ref, dn_ref, dt_ref, tdb_ref, vec_ref, bias_ref, chan_up_ref, chan_down_ref,
    mixed_out, grad_out, gup_out, gdn_out, small_out,
    pat, cot, cot_in, stats, stats_in, means, means2, tin, th, tslope, msend, mrecv, rows_m, rows_n, inv2, vec_in,
    xs_all, gs_all, w_up, w_dn, w_b, hid_s, pg_s, out_acc, ng_acc, xch_send, ng_in, out_in,
    blow, gacc, vecs,
    gm, gb, rx, yb, ry, ryo, zb, rz, rzo, fin_up, fin, small_send, small_in, small_z,
    loc_sem, send_sem, recv_sem,
):
    z = lax.axis_index("dp")
    y = lax.axis_index("chan")
    h = lax.axis_index("hid")
    c = h % 2
    x = h // 2
    S, PS, L, OWN, IM, X, C = o.s, o.ps, o.l, o.own, o.images, o.xs, o.chunks
    width = float(o.d)
    here = y * o.hid + h
    bit = z % 2
    half_l = L // 2

    def dev(zz=None, yy=None, xx=None, cc=None):
        zz = z if zz is None else zz
        yy = y if yy is None else yy
        xx = x if xx is None else xx
        cc = c if cc is None else cc
        return (zz, yy, xx * 2 + cc)

    partner = dev(yy=1 - y)
    sibling = dev(cc=1 - c)
    z_pair = dev(zz=z + 1 - 2 * bit)
    counter = [0]

    def take(count=1):
        base = counter[0]
        counter[0] += count
        return base

    def remote(src, dst, device, index=None):
        index = take() if index is None else index
        return pltpu.make_async_remote_copy(
            src_ref=src, dst_ref=dst, send_sem=send_sem.at[index], recv_sem=recv_sem.at[index],
            device_id=device, device_id_type=MESH,
        )

    def send(src, dst, device):
        copy = remote(src, dst, device)
        copy.start()
        return copy

    barrier = pltpu.get_barrier_semaphore()
    for step in range(1, o.plane):
        there = (here + step) % o.plane
        pl.semaphore_signal(barrier, inc=1, device_id=(z, there // o.hid, there % o.hid), device_id_type=MESH)
    for step in range(1, o.dp):
        pl.semaphore_signal(barrier, inc=1, device_id=((z + step) % o.dp, y, h), device_id_type=MESH)

    loads = []

    def load(src, dst):
        copy = pltpu.make_async_copy(src, dst, loc_sem.at[len(loads)])
        loads.append(copy)
        copy.start()
        return copy

    load_pat = load(patches_ref, pat)
    load_cot = load(cot_ref, cot)
    load_up0 = load(chan_up_ref.at[pl.ds(pl.multiple_of(y * L, L), L)], w_up.at[0, pl.ds(0, L)])
    load_up1 = load(chan_up_ref.at[pl.ds(pl.multiple_of((1 - y) * L, L), L)], w_up.at[0, pl.ds(L, L)])
    load_dn = load(chan_down_ref, w_dn.at[0, :, pl.ds(0, L)])
    load_b = load(bias_ref, w_b.at[0])

    pad = PS - S
    pad_row = lax.broadcasted_iota(jnp.int32, (pad, L), 0)
    one_row = jnp.where(pad_row == 0, 1.0, 0.0).astype(BF)
    for j in range(IM):
        tin[j, S:PS, :] = one_row
    for i in range(OWN):
        xs_all[c, i, S:PS, :] = jnp.zeros((pad, o.d), BF)
        gs_all[c, i, S:PS, :] = jnp.zeros((pad, o.d), BF)
        rows_n[i, S:PS, :] = jnp.zeros((pad, o.d), F32)
        rows_m[i, S:PS, :] = jnp.zeros((pad, o.d), F32)
        inv2[i, S:PS, :] = jnp.zeros((pad, 1), F32)
        msend[i, S:PS, :] = jnp.zeros((pad, L), BF)
    vecs[...] = jnp.zeros(vecs.shape, F32)
    gacc[...] = jnp.zeros(gacc.shape, F32)

    lane = lax.broadcasted_iota(jnp.int32, (S, 128), 1)
    load_pat.wait()

    def note(table, j, first, second):
        table = jnp.where(lane == j, first, table)
        return jnp.where(lane == j + 8, second, table)

    def across(table):
        rest = jnp.zeros((o.wide - S, 128), F32)
        return jnp.concatenate([table, rest], 0).T[:16]

    def along(table):
        return jnp.concatenate([table, jnp.zeros((112, o.wide), F32)], 0).T

    def sums_of(j, table):
        v = pat[j].astype(F32)
        return note(table, j, jnp.sum(v, -1, keepdims=True), jnp.sum(v * v, -1, keepdims=True))

    stats[0] = across(lax.fori_loop(0, IM, sums_of, jnp.zeros((S, 128), F32)))

    pl.semaphore_wait(barrier, o.plane - 1 + o.dp - 1)

    copy_stats = send(stats.at[0], stats_in.at[0], partner)
    copy_vec = send(vec_ref, vec_in, partner)
    near = pl.ds(bit * L, L)
    near_from = pl.ds(pl.multiple_of(((y + bit) % 2) * L, L), L)
    copy_b = {step: send(bias_ref, w_b.at[step], dev(xx=(x + step) % X)) for step in range(1, X)}
    copy_w = {}
    copy_f = {}

    def weight_spans(step, part):
        cols = pl.ds(part * L, L)
        rows_dn = pl.ds(pl.multiple_of(part * L + bit * half_l, 16), half_l)
        return (
            (chan_up_ref.at[near_from, cols], w_up.at[step, near, cols], y),
            (chan_down_ref.at[rows_dn], w_dn.at[step, rows_dn, pl.ds(0, L)], y),
            (chan_down_ref.at[rows_dn], w_dn.at[step, rows_dn, pl.ds(L, L)], 1 - y),
        )

    def fetch(part, which):
        for step in range(1, X):
            for n in which:
                src, dst, yy = weight_spans(step, part)[n]
                copy_w[step, part, n] = send(src, dst, dev(xx=(x + step) % X, yy=yy))

    def hand_on(part, which):
        for step in range(1, X):
            for n in which:
                dst = weight_spans(step, part)[n][1]
                copy_w[step, part, n].wait()
                copy_f[step, part, n] = send(dst, dst, z_pair)

    fetch(0, (0,))
    copy_cot = send(cot_ref.at[pl.ds((1 - y) * OWN, OWN)], cot_in, partner)
    fetch(0, (1, 2))

    copy_stats.wait()
    total = (stats[0] + stats_in[0]) * (1.0 / width)
    mean, square = total[:8], total[8:]
    means[...] = along(jnp.concatenate([mean, lax.rsqrt(square - mean * mean + EPS)], 0))

    def column(table, j):
        return jnp.sum(jnp.where(lane == j, table, 0.0), -1, keepdims=True)

    first_gain = vec_ref[0:1, :]
    first_shift = vec_ref[1:2, :]

    def first_norm(j):
        table = means[:S, :]
        inv_one = column(table, j + 8)
        return (pat[j].astype(F32) - column(table, j)) * inv_one, inv_one

    def token_forward(j):
        normed, _ = first_norm(j)
        tin[j, :S, :] = (normed * first_gain + first_shift).astype(BF)
        value, slope = gelu_pair(nn(ut_ref[...], tin[j]))
        th[j] = value.astype(BF)
        tslope[j] = slope.astype(BF)
        back = nn(dt_ref[...], th[j])
        return pat[j].astype(F32) + back[:S] + tdb_ref[:S, :]

    mixed_sems = take(OWN)

    def copy_mixed(i):
        return remote(msend.at[i], mrecv.at[i], partner, mixed_sems + i)

    @pl.loop(0, OWN)
    def _(i):
        msend[i, :S, :] = token_forward((1 - y) * OWN + i).astype(BF)
        copy_mixed(i).start()

    @pl.loop(0, OWN)
    def _(i):
        rows_m[i, :S, :L] = token_forward(y * OWN + i)

    hand_on(0, (0,))
    load_cot.wait()
    copy_cot.wait()
    live = live_ref[0]

    def keep_of(j):
        return jnp.where(j < live, 1.0, 0.0).astype(F32)

    @pl.loop(0, OWN)
    def _(i):
        keep = keep_of(y * OWN + i)
        gs_all[c, i, :S, :L] = (cot[y * OWN + i].astype(F32) * keep).astype(BF)
        gs_all[c, i, :S, L:] = (cot_in[i].astype(F32) * keep).astype(BF)

    copy_gs = send(gs_all.at[c], gs_all.at[c], sibling)
    hand_on(0, (1, 2))
    for part in range(1, C):
        fetch(part, (0, 1))

    copy_vec.wait()
    both = [jnp.concatenate([vec_ref[n:n + 1, :], vec_in[n:n + 1, :]], axis=1) for n in range(2, 5)]
    second_gain, second_shift, down_bias = both
    row_sems = take(OWN)

    def copy_rows(i):
        return remote(xs_all.at[c, i], xs_all.at[c, i], sibling, row_sems + i)

    @pl.loop(0, OWN)
    def _(i):
        copy_mixed(i).wait()
        rows_m[i, :S, L:] = mrecv[i, :S, :].astype(F32)
        v = rows_m[i, :S, :]
        mean = jnp.sum(v, -1, keepdims=True) * (1.0 / width)
        spread = jnp.sum(v * v, -1, keepdims=True) * (1.0 / width) - mean * mean
        inv_two = lax.rsqrt(spread + EPS)
        normed = (v - mean) * inv_two
        inv2[i, :S, :] = inv_two
        rows_n[i, :S, :] = normed
        xs_all[c, i, :S, :] = (normed * second_gain + second_shift).astype(BF)
        copy_rows(i).start()

    for part in range(1, C):
        fetch(part, (2,))
    copy_dn2 = {}

    def fetch_dn2(part):
        span = pl.ds(part * L, L)
        copy_dn2[part] = send(chan_down_ref.at[span], w_dn.at[0, span, pl.ds(L, L)], partner)

    fetch_dn2(0)
    load_up0.wait()
    load_up1.wait()
    load_dn.wait()
    load_b.wait()
    copy_gs.wait()
    for part in range(1, C):
        hand_on(part, (0, 1))

    @pl.loop(0, OWN)
    def _(i):
        copy_rows(i).wait()

    ready = {}

    def levels():
        start, count, used = 0, o.dp, 0
        for level in range(o.levels):
            side_bit = (z // (1 << level)) % 2
            peer = dev(zz=z + (1 - 2 * side_bit) * (1 << level))
            count //= 2
            yield start + side_bit * count, start + (1 - side_bit) * count, count, used, peer
            start = start + side_bit * count
            used += count

    def add(part, kind, half, span, *terms):
        mine = gm[part, kind, half, span]
        for term in terms:
            mine = mine + term.astype(F32)
        gm[part, kind, half, span] = mine

    everything = pl.ds(0, o.dp)

    def gather(part, kind):
        halves = 2 if kind == 0 else 1
        done = fin_up if kind == 0 else fin
        own = pl.ds(my_segment(), 1)
        done[part, 0, own] = gm[part, kind, 0, own].astype(BF)
        if kind == 0:
            copy = send(fin_up.at[part, 0, own], fin_up.at[part, 1, own], partner)
            yield
            copy.wait()
        for keep_at, _, count, _, peer in reversed(list(levels())):
            copies = []
            for half in range(halves):
                span = done.at[part, half, pl.ds(keep_at, count)]
                copies.append(send(span, span, peer))
            yield
            for copy in copies:
                copy.wait()
        if kind == 0:
            gup_out[part, y] = fin_up[part, 0]
            gup_out[part, 1 - y] = fin_up[part, 1]
        else:
            gdn_out[part] = fin[part, 0]

    def slot(part, kind, half):
        return o.slots.index((part, kind, half))

    def reduce_z(part, kind, halves):
        for keep_at, send_at, count, used, peer in levels():
            span = pl.ds(used, count)
            copies = []
            for half in range(halves):
                here_z = slot(part, kind, half)
                zb[here_z, span] = gm[part, kind, half, pl.ds(send_at, count)].astype(BF)
                copies.append(send(zb.at[here_z, span], rz.at[here_z, span], peer))
            yield
            for half in range(halves):
                copies[half].wait()
                add(part, kind, half, pl.ds(keep_at, count), rz[slot(part, kind, half), span])

    def my_segment():
        return list(levels())[-1][0]

    def chunk_xyz(part, kind):
        copies = [send(gb.at[n, part, kind], rx.at[n, part, kind], dev(xx=(x + X - 1 - n) % X)) for n in range(X - 1)]
        yield
        for n in range(X - 1):
            copies[n].wait()
        for half in (1, 0):
            add(part, kind, half, everything, *[rx[n, part, kind, half] for n in range(X - 1)])
            if half:
                yb[part, kind] = gm[part, kind, 1].astype(BF)
                copy = send(yb.at[part, kind], ry.at[part, kind], partner)
        yield
        copy.wait()
        add(part, kind, 0, everything, ry[part, kind])
        yield from reduce_z(part, kind, 1)
        yield from gather(part, kind)

    def chunk_yxz(part, kind):
        copies = [send(gb.at[n, part, kind, 1], ryo.at[n, part, kind], partner) for n in range(X - 1)]
        yield
        for n in range(X - 1):
            copies[n].wait()
            mine = gb[n, part, kind, 0].astype(F32) + ryo[n, part, kind].astype(F32)
            gb[n, part, kind, 0] = mine.astype(BF)
            copies[n] = send(gb.at[n, part, kind, 0], rx.at[n, part, kind, 0], dev(xx=(x + X - 1 - n) % X))
        yb[part, kind] = gm[part, kind, 1].astype(BF)
        copy = send(yb.at[part, kind], ry.at[part, kind], partner)
        yield
        copy.wait()
        for n in range(X - 1):
            copies[n].wait()
        add(part, kind, 0, everything, ry[part, kind], *[rx[n, part, kind, 0] for n in range(X - 1)])
        yield from reduce_z(part, kind, 1)
        yield from gather(part, kind)

    def chunk_zxy(part, kind):
        for keep_at, send_at, count, used, peer in levels():
            copies = {}
            span = pl.ds(used, count)
            for n in range(X - 1):
                for half in range(2):
                    src = gb.at[n, part, kind, half, pl.ds(send_at, count)]
                    copies[n, half] = send(src, rzo.at[n, o.firsts.index((part, kind)), half, span], peer)
            yield
            for n in range(X - 1):
                for half in range(2):
                    copies[n, half].wait()
                    keep = pl.ds(keep_at, count)
                    mine = gb[n, part, kind, half, keep].astype(F32) + rzo[n, o.firsts.index((part, kind)), half, span].astype(F32)
                    gb[n, part, kind, half, keep] = mine.astype(BF)
        at = pl.ds(my_segment(), 1)
        copies = []
        for n in range(X - 1):
            span = gb.at[n, part, kind, :, at]
            copies.append(send(span, rx.at[n, part, kind, :, at], dev(xx=(x + X - 1 - n) % X)))
        yield from reduce_z(part, kind, 2)
        for copy in copies:
            copy.wait()
        for half in (1, 0):
            add(part, kind, half, at, *[rx[n, part, kind, half, at] for n in range(X - 1)])
            if half:
                yb[part, kind, at] = gm[part, kind, 1, at].astype(BF)
                copy = send(yb.at[part, kind, at], ry.at[part, kind, at], partner)
        yield
        copy.wait()
        add(part, kind, 0, at, ry[part, kind, at])
        yield from gather(part, kind)

    pipes = {}

    def begin(part, kind):
        pipes[part, kind] = o.ways[part % len(o.ways)][kind]
        pipes[part, kind] = {"xyz": chunk_xyz, "yxz": chunk_yxz, "zxy": chunk_zxy}[pipes[part, kind]](part, kind)
        step_of((part, kind))

    def step_of(name):
        if name in pipes:
            try:
                next(pipes[name])
            except StopIteration:
                del pipes[name]

    def at(*point):
        for name in o.plan.get(point, ()):
            step_of(name)

    rows = OWN * PS
    first = True

    def weight_grad(kind, half):
        lanes = pl.ds(half * L, L)
        if kind == 0:
            grad = tn(xs_all[:, :, :, lanes].reshape(2 * rows, L), pg_s[...].reshape(2 * rows, L))
        else:
            grad = tn(hid_s[...].reshape(2 * rows, L), gs_all[:, :, :, lanes].reshape(2 * rows, L))
        return grad.reshape(o.dp, o.seg, L)

    for part in range(C):
        for step in list(range(1, X)) + [0]:
            if step:
                if part == 0:
                    copy_b[step].wait()
                for n in range(3):
                    copy_f[step, part, n].wait()
            else:
                copy_dn2[part].wait()
            cols = pl.ds(part * L, L)

            def side(cc, total, first=first, step=step, cols=cols):
                xin = xs_all[cc].reshape(rows, o.d)
                gin = gs_all[cc].reshape(rows, o.d)
                value, slope = gelu_pair(nn(xin, w_up[step, :, cols]) + w_b[step, 0:1, cols])
                hidden = value.astype(BF)
                hid_s[cc] = hidden
                down = w_dn[step, cols, :]
                add_out = nn(hidden, down)
                pre = (nt(gin, down) * slope).astype(BF)
                pg_s[cc] = pre
                add_ng = nt(pre, w_up[step, :, cols])
                if first:
                    out_acc[cc] = add_out
                    ng_acc[cc] = add_ng
                else:
                    out_acc[cc] += add_out
                    ng_acc[cc] += add_ng
                return total + jnp.sum(pre.astype(F32), 0, keepdims=True)

            up_bias_grad = lax.fori_loop(0, 2, side, jnp.zeros((1, L), F32))
            if step == 1:
                if part + 1 < C:
                    hand_on(part + 1, (2,))
                    fetch_dn2(part + 1)
            owner = ((x + X - step) % X * 2 + c) * C + part
            vecs[3 + owner, 0:1, :] = up_bias_grad
            first = False
            if step in (0, X - 1):
                at("M" if step == 0 else "O", part, "side")
            if step == 0 and part == C - 1:
                xch_send[0] = ng_acc[1 - c].astype(BF)
                copy_ng = send(xch_send.at[0], ng_in, sibling)
                xch_send[1] = out_acc[1 - c].astype(BF)
                copy_out = send(xch_send.at[1], out_in, sibling)
            for kind in range(2):
                for half in range(2):
                    if step:
                        gb[step - 1, part, kind, half] = weight_grad(kind, half).astype(BF)
                    else:
                        gm[part, kind, half] = weight_grad(kind, half)
                if step == X - 1:
                    begin(part, kind)
            if step in (0, X - 1):
                at("M" if step == 0 else "O", part, "grad")

    res_sems = take(OWN)

    def copy_res(i):
        return remote(mrecv.at[i], blow.at[y * OWN + i], partner, res_sems + i)

    copy_ng.wait()

    def residual(i, sums):
        block = pl.ds(pl.multiple_of(i * PS, 16), PS)
        ng = ng_acc[c, block, :] + ng_in[block, :].astype(F32)
        normed = rows_n[i]
        back = gs_all[c, i].astype(F32)
        sums = (
            sums[0] + jnp.sum(ng * normed, 0, keepdims=True),
            sums[1] + jnp.sum(ng, 0, keepdims=True),
            sums[2] + jnp.sum(back, 0, keepdims=True),
        )
        q = ng * second_gain
        m1 = jnp.sum(q, -1, keepdims=True) * (1.0 / width)
        m2 = jnp.sum(q * normed, -1, keepdims=True) * (1.0 / width)
        res = (back + inv2[i] * (q - m1 - normed * m2)).astype(BF)
        mrecv[i] = res[:, L:]
        copy_res(i).start()
        blow[y * OWN + i] = res[:, :L]
        return sums

    zero = jnp.zeros((1, o.d), F32)
    sums = lax.fori_loop(0, OWN, residual, (zero, zero, zero))
    for n in range(3):
        vecs[0, 1 + 2 * n:2 + 2 * n, :] = jnp.where(y == 0, sums[n][:, :L], sums[n][:, L:])
        vecs[0, 2 + 2 * n:3 + 2 * n, :] = jnp.where(y == 0, sums[n][:, L:], sums[n][:, :L])
    at("residual")

    ones = jnp.ones((16, L), BF)

    def scaled(j):
        return j // OWN, pl.ds(pl.multiple_of(j % OWN * PS, 16), PS), pl.ds(0, L)

    def token_backward(j, carry):
        table, sum_gain, sum_shift, sum_bias = carry
        low = blow[j]
        grad = (nn(dn_ref[...], low) * tslope[j].astype(F32)).astype(BF)
        gacc[0] += nt(tin[j], grad)
        gacc[1] += nt(low, th[j])
        sum_bias = sum_bias + nt(ones, low)
        back = nn(up_ref[...], grad)
        normed, _ = first_norm(j)
        sum_gain = sum_gain + jnp.sum(back[:S] * normed, 0, keepdims=True)
        sum_shift = sum_shift + jnp.sum(back[:S], 0, keepdims=True)
        back = back * first_gain
        ng_acc[scaled(j)] = back
        back = back[:S]
        table = note(table, j, jnp.sum(back, -1, keepdims=True), jnp.sum(back * normed, -1, keepdims=True))
        return table, sum_gain, sum_shift, sum_bias

    carry = (jnp.zeros((S, 128), F32), jnp.zeros((1, L), F32), jnp.zeros((1, L), F32), jnp.zeros((16, PS), F32))
    carry = lax.fori_loop(0, OWN, lambda i, t: token_backward(y * OWN + i, t), carry)
    at("token own")

    def later(i, t):
        copy_res(i).wait()
        return token_backward((1 - y) * OWN + i, t)

    table, sum_gain, sum_shift, sum_bias = lax.fori_loop(0, OWN, later, carry)
    stats[1] = across(table)
    copy_stats2 = send(stats.at[1], stats_in.at[1], partner)
    vecs[0, 0:1, :PS] = sum_bias[0:1, :]
    vecs[1 + y, 0:1, :] = sum_gain
    vecs[1 + y, 1:2, :] = sum_shift

    def piece(n):
        return pl.ds(pl.multiple_of(n * o.piece, 16), o.piece)

    def plane_peers():
        for step in range(1, o.plane):
            there = (here + step) % o.plane
            yield step, there, (z, there // o.hid, there % o.hid)

    small_send[0:PS, :] = gacc[0].astype(BF)
    small_send[PS:2 * PS, :] = gacc[1].astype(BF)
    small_send[o.vec_row:, :] = vecs[...].reshape(8 * o.groups, L).astype(BF)

    def reduce_small():
        copies = [send(small_send.at[piece(there)], small_in.at[n - 1], peer) for n, there, peer in plane_peers()]
        yield
        for copy in copies:
            copy.wait()
        mine = small_send[piece(here), :].astype(F32)
        for n in range(1, o.plane):
            mine = mine + small_in[n - 1].astype(F32)
        small_z[z] = mine.astype(BF)
        copies = [send(small_z.at[z], small_z.at[z], ((z + n) % o.dp, y, h)) for n in range(1, o.dp)]
        yield
        for copy in copies:
            copy.wait()
        mine = small_z[0].astype(F32)
        for n in range(1, o.dp):
            mine = mine + small_z[n].astype(F32)
        small_out[piece(here), :] = mine.astype(BF)
        copies = [send(small_out.at[piece(here)], small_out.at[piece(here)], peer) for _, _, peer in plane_peers()]
        yield
        for copy in copies:
            copy.wait()

    pipes["small"] = reduce_small()
    step_of("small")
    at("token other")

    copy_stats2.wait()
    means2[...] = along((stats[1] + stats_in[1]) * (1.0 / width))

    @pl.loop(0, IM)
    def _(j):
        normed, inv_one = first_norm(j)
        grad = ng_acc[scaled(j)][:S]
        grad = grad - column(means2[:S, :], j) - normed * column(means2[:S, :], j + 8)
        grad_out[j, :S, :] = (blow[j, :S, :].astype(F32) + inv_one * grad).astype(BF)
        grad_out[j, S:, :] = jnp.zeros((PS - S, L), BF)

    at("norm")

    copy_out.wait()
    mixed_sems2 = take(OWN)

    def copy_mo(i):
        return remote(msend.at[i], mixed_out.at[y * OWN + i], partner, mixed_sems2 + i)

    @pl.loop(0, OWN)
    def _(i):
        block = pl.ds(pl.multiple_of(i * PS, 16), PS)
        branch = out_acc[c, block, :] + out_in[block, :].astype(F32) + down_bias
        result = (keep_of(y * OWN + i) * (rows_m[i] + branch)).astype(BF)
        msend[i] = result[:, L:]
        copy_mo(i).start()
        mixed_out[y * OWN + i] = result[:, :L]

    at("end")
    while pipes:
        for name in list(pipes):
            step_of(name)

    @pl.loop(0, OWN)
    def _(i):
        copy_mo(i).wait()


def block_call(o, live, patches, cot, ut, up, dn, dt, tdb, vec, bias, chan_up, chan_down):
    I, S, PS, L, OWN, D, X, C = o.images, o.s, o.ps, o.l, o.own, o.d, o.xs, o.chunks
    any_spec = pl.BlockSpec(memory_space=pl.ANY)
    vmem = pl.BlockSpec(memory_space=pltpu.VMEM)
    rows = OWN * PS
    block = (o.dp, o.seg, L)
    less = (o.dp - 1, o.seg, L)
    copies = 16 + 4 * OWN + (X - 1) * (1 + 6 * C) + C + 2 * (o.plane - 1) + o.dp - 1
    copies += 2 * C * ((X - 1) * (2 + 2 * o.levels) + 4 * o.levels + 2) + C
    outs = [
        jax.ShapeDtypeStruct((I, PS, L), BF),
        jax.ShapeDtypeStruct((I, PS, L), BF),
        jax.ShapeDtypeStruct((C, 2, o.dp, o.seg, L), BF),
        jax.ShapeDtypeStruct((C, o.dp, o.seg, L), BF),
        jax.ShapeDtypeStruct((o.small, L), BF),
    ]
    scratch = [
        ((I, S, L), BF), ((I, S, L), BF), ((OWN, S, L), BF),
        ((2, 16, o.wide), F32), ((2, 16, o.wide), F32), ((o.wide, 128), F32), ((o.wide, 128), F32),
        ((I, PS, L), BF), ((I, o.ds, L), BF), ((I, o.ds, L), BF),
        ((OWN, PS, L), BF), ((OWN, PS, L), BF),
        ((OWN, PS, D), F32), ((OWN, PS, D), F32), ((OWN, PS, 1), F32), ((8, L), F32),
        ((2, OWN, PS, D), BF), ((2, OWN, PS, D), BF),
        ((X, D, o.f), BF), ((X, o.f, D), BF), ((X, 8, o.f), F32),
        ((2, rows, L), BF), ((2, rows, L), BF), ((2, rows, D), F32), ((2, rows, D), F32),
        ((2, rows, D), BF), ((rows, D), BF), ((rows, D), BF),
        ((I, PS, L), BF),
        ((2, PS, L), F32), ((o.groups, 8, L), F32),
        ((C, 2, 2) + block, F32), ((X - 1, C, 2, 2) + block, BF), ((X - 1, C, 2, 2) + block, BF),
        ((C, 2) + block, BF), ((C, 2) + block, BF), ((X - 1, C, 2) + block, BF),
        ((len(o.slots),) + less, BF), ((len(o.slots),) + less, BF),
        ((X - 1, max(1, len(o.firsts)), 2) + (less if o.firsts else (1, 16, 128)), BF),
        ((C, 2) + block, BF), ((C, 1) + block, BF),
        ((o.small, L), BF), ((o.plane - 1, o.piece, L), BF), ((o.dp, o.piece, L), BF),
    ]
    return pl.pallas_call(
        functools.partial(kernel, o),
        out_shape=outs,
        in_specs=[pl.BlockSpec(memory_space=pltpu.SMEM), any_spec, any_spec] + [vmem] * 7 + [any_spec] * 2,
        out_specs=[vmem] * 5,
        scratch_shapes=[pltpu.VMEM(shape, kind) for shape, kind in scratch]
        + [pltpu.SemaphoreType.DMA((8,)), pltpu.SemaphoreType.DMA((copies,)), pltpu.SemaphoreType.DMA((copies,))],
        compiler_params=pltpu.CompilerParams(
            collective_id=1, has_side_effects=True, vmem_limit_bytes=63 * 2**20
        ),
        name="mixer_block",
    )(live, patches, cot, ut, up, dn, dt, tdb, vec, bias, chan_up, chan_down)


def body(
    o,
    patches,
    cotangent,
    live_images,
    first_gain,
    first_shift,
    token_up,
    token_up_bias,
    token_down,
    token_down_bias,
    second_gain,
    second_shift,
    chan_up,
    chan_up_bias,
    chan_down,
    chan_down_bias,
):
    S, PS, L = o.s, o.ps, o.l
    rest = PS - S
    up = jnp.pad(token_up, ((0, rest), (0, 0)))
    ut = jnp.concatenate([token_up, token_up_bias[None], jnp.zeros((rest - 1, o.ds), BF)], 0).T
    dn = jnp.pad(token_down, ((0, 0), (0, rest)))
    dt = jnp.pad(token_down.T, ((0, rest), (0, 0)))
    tdb = jnp.pad(token_down_bias.astype(F32), (0, rest))[:, None]
    vec = jnp.stack([first_gain, first_shift, second_gain, second_shift, chan_down_bias] + [jnp.zeros((L,), BF)] * 3)
    bias = jnp.broadcast_to(chan_up_bias.astype(F32)[None], (8, o.f))
    mixed, grad, gup, gdn, small = block_call(
        o, live_images, patches, cotangent, ut, up, dn, dt, tdb, vec.astype(F32), bias, chan_up, chan_down
    )
    y = lax.axis_index("chan")
    h = lax.axis_index("hid")
    small = small.astype(F32)
    groups = small[o.vec_row:].reshape(o.groups, 8, L)

    def pick(at, row):
        return lax.dynamic_slice_in_dim(groups[:, row], at, 1, 0)[0]

    def pick_half(row):
        return lax.dynamic_slice_in_dim(groups[0], row + y, 1, 0)[0]

    return (
        mixed[:, :S],
        grad[:, :S],
        pick(1 + y, 0),
        pick(1 + y, 1),
        small[:S],
        small[S],
        small[PS:PS + S].T,
        groups[0, 0, :S],
        pick_half(1),
        pick_half(3),
        gup.reshape(o.chunks, 2, L, L).transpose(1, 2, 0, 3).reshape(o.d, o.f).astype(F32),
        lax.dynamic_slice_in_dim(groups[:, 0], 3 + h * o.chunks, o.chunks, 0).reshape(o.f),
        gdn.reshape(o.f, L).astype(F32),
        pick_half(5),
    )


def solution(mesh):
    in_specs = (
        P(("dp", "hid"), None, "chan"),
        P(("dp", "hid"), None, "chan"),
        P(("dp", "hid")),
        P("chan"),
        P("chan"),
        P(),
        P(),
        P(),
        P(),
        P("chan"),
        P("chan"),
        P(None, "hid"),
        P("hid"),
        P("hid", "chan"),
        P("chan"),
    )
    out_specs = (
        P(("dp", "hid"), None, "chan"),
        P(("dp", "hid"), None, "chan"),
        P("chan"),
        P("chan"),
        P(),
        P(),
        P(),
        P(),
        P("chan"),
        P("chan"),
        P(None, "hid"),
        P("hid"),
        P("hid", "chan"),
        P("chan"),
    )

    def whole(*args):
        shape = dict(mesh.shape)
        patches, token_up, chan_up = args[0].shape, args[5].shape, args[11].shape
        local = (patches[0] // (shape["dp"] * shape["hid"]), patches[1], patches[2] // shape["chan"])
        o = Sizes(shape, local, (chan_up[0], chan_up[1] // shape["hid"]), token_up)
        mapped = jax.shard_map(
            functools.partial(body, o), mesh=mesh, in_specs=in_specs, out_specs=out_specs, check_vma=False
        )
        return mapped(*args)

    return whole
```

time: 249 us -> 162 us (0.65)
  Pallas kernels: 227 us -> 138 us
    pallas_call x1, Pallas kernels: 227 us -> 138 us  [block_call(): pl.pallas_call(functools.partial(kernel, o), out_shape=outs, in_specs=[pl...]
where the time goes in v2:
time: 162 us; the launch traced here: 160 us
  Pallas kernels  138 us (85%)
  local copies, waits for them, and re-layouts  17.2 us (11%)
  other arithmetic  2.86 us (2%)
    pallas_call x1, Pallas kernels, block_call(): pl.pallas_call(functools.partial(kernel, o), out_shape=outs, in_specs=[pl...  138 us

profile of v2, /device:TPU:0, one launch (start us, length us, event | category | flops | bytes accessed | tf_op | source)
XLA Modules:
  0.0 159.7 jit_solution(4907632736030402262)
XLA Ops:
  1.3 0.8 broadcast_in_dim.23
  2.2 1.1 copy.32
  3.3 0.1 pad.22.clone
  3.4 0.8 maximum_bitcast_fusion.ut_ref
  4.2 1.6 pad.16.up_ref
  5.8 0.1 copy.34
  5.9 0.7 pad.17.dn_ref
  6.6 0.7 pad.18.dt_ref
  7.3 0.8 copy.35.tdb_ref
  8.2 0.6 convert_element_type.35.vec_ref
  8.8 0.6 broadcast_in_dim.21.bias_ref
  9.5 138.1 %mixer_block.1 = (bf16[6,208,384]{2,1,0:T(8,128)(2,1)}, bf16[6,208,384]{2,1,0:T(8,128)(2,1)}, bf16[2,2,4,96,384]{4,3,2,1,0:T(8,128)(2,1)}, bf16[2,4,96,384]{3,2,1,0:T(8,128)(2,1)}, bf16[512,384]{1,0:T(8,128)(2,1)}) custom-call(s32[1]{0:T(128)S(6)} %copy.38.live_ref, bf16[6,196,384]{2,1,0:T(8,128)(2,1)} %patches_ref.1, bf16[6,196,384]{2,1,0:T(8,128)(2,1)} %cot_ref.1, ...), custom_call_target="tpu_custom_call" | custom-call | tf_op jit(solution)/shard_map/mixer_block/pallas_call | solution.py:726
  147.6 2.3 %slice.35 = bf16[6,196,384]{2,1,0:T(8,128)(2,1)} slice(bf16[6,208,384]{2,1,0:T(8,128)(2,1)} %get-tuple-element.19), slice={[0:6], [0:196], [0:384]} | slice | bytes 1806336 | tf_op jit(solution)/shard_map/slice | solution.py:782
  149.9 1.0 slice.36
  151.0 0.6 dynamic-slice_reduce_fusion.4
  151.6 0.7 slice.48
  152.4 0.6 dynamic-slice_reduce_fusion.1
  153.0 0.7 slice_bitcast_fusion
  153.7 0.6 slice.51
  154.3 0.3 convert_bitcast_fusion
  154.6 1.8 %copy.36 = f32[2,384,2,384]{3,2,1,0:T(2,128)S(1)} copy(f32[2,384,2,384]{3,1,0,2:T(8,128)S(1)} %convert_bitcast_fusion) | data formatting | bytes 4718592 | tf_op jit(solution)/shard_map/convert_element_type | solution.py:792
  156.4 1.6 copy.37
  158.0 0.6 reshape.55
  158.6 1.1 bitcast_convert_fusion
  (39 shorter events, 0.3 us)
Async XLA Ops:
  0.6 5.1 %copy-start.3 = (bf16[384,196]{0,1:T(8,128)(2,1)S(1)}, bf16[384,196]{0,1:T(8,128)(2,1)}, u32[]{:S(2)}) copy-start(bf16[384,196]{0,1:T(8,128)(2,1)} %param.22) | copy-start | bytes 451588
  0.7 6.6 %copy-start.11 = (bf16[196]{0:T(256)(128)(2,1)S(1)}, bf16[196]{0:T(256)(128)(2,1)}, u32[]{:S(2)}) copy-start(bf16[196]{0:T(256)(128)(2,1)} %param.23) | copy-start | bytes 1180
  2.1 5.9 %copy-start.6 = (bf16[384]{0:T(512)(128)(2,1)S(1)}, bf16[384]{0:T(512)(128)(2,1)}, u32[]{:S(2)}) copy-start(bf16[384]{0:T(512)(128)(2,1)} %param.18) | copy-start | bytes 2308
  2.2 5.9 %copy-start.7 = (bf16[384]{0:T(512)(128)(2,1)S(1)}, bf16[384]{0:T(512)(128)(2,1)}, u32[]{:S(2)}) copy-start(bf16[384]{0:T(512)(128)(2,1)} %param.19) | copy-start | bytes 2308
  2.2 5.9 %copy-start.8 = (bf16[384]{0:T(512)(128)(2,1)S(1)}, bf16[384]{0:T(512)(128)(2,1)}, u32[]{:S(2)}) copy-start(bf16[384]{0:T(512)(128)(2,1)} %param.24) | copy-start | bytes 2308
  2.2 5.9 %copy-start.9 = (bf16[384]{0:T(512)(128)(2,1)S(1)}, bf16[384]{0:T(512)(128)(2,1)}, u32[]{:S(2)}) copy-start(bf16[384]{0:T(512)(128)(2,1)} %param.25) | copy-start | bytes 2308
  2.2 6.0 %copy-start.10 = (bf16[384]{0:T(512)(128)(2,1)S(1)}, bf16[384]{0:T(512)(128)(2,1)}, u32[]{:S(2)}) copy-start(bf16[384]{0:T(512)(128)(2,1)} %param.29) | copy-start | bytes 2308
  2.2 6.6 %copy-start.5 = (bf16[768]{0:T(1024)(128)(2,1)S(1)}, bf16[768]{0:T(1024)(128)(2,1)}, u32[]{:S(2)}) copy-start(bf16[768]{0:T(1024)(128)(2,1)} %param.27) | copy-start | bytes 4612
  147.6 2.3 %copy-start.2 = (bf16[6,208,384]{2,1,0:T(8,128)(2,1)S(1)}, bf16[6,208,384]{2,1,0:T(8,128)(2,1)}, u32[]{:S(2)}) copy-start(bf16[6,208,384]{2,1,0:T(8,128)(2,1)} %get-tuple-element.20) | copy-start | bytes 2875396
  149.9 1.0 copy-start
  150.9 3.4 %copy-start.1 = (bf16[2,2,4,96,384]{4,3,2,1,0:T(8,128)(2,1)S(1)}, bf16[2,2,4,96,384]{4,3,2,1,0:T(8,128)(2,1)}, u32[]{:S(2)}) copy-start(bf16[2,2,4,96,384]{4,3,2,1,0:T(8,128)(2,1)} %get-tuple-element.22) | copy-start | bytes 3538948
  156.4 2.2 %copy-start.4 = (bf16[2,4,96,384]{3,2,1,0:T(8,128)(2,1)S(1)}, bf16[2,4,96,384]{3,2,1,0:T(8,128)(2,1)}, u32[]{:S(2)}) copy-start(bf16[2,4,96,384]{3,2,1,0:T(8,128)(2,1)} %get-tuple-element.23) | copy-start | bytes 1769476

commit v3 on v2

v3 whole, which is shorter than its diff:
```python
import functools

import jax
import jax.numpy as jnp
from jax import lax
from jax.experimental import pallas as pl
from jax.experimental.pallas import tpu as pltpu
from jax.sharding import PartitionSpec as P

EPS = 1e-06
BF = jnp.bfloat16
F32 = jnp.float32
MESH = pl.DeviceIdType.MESH
TANH_A = 0.7978845608028654
TANH_B = TANH_A * 0.044715


def nn(left, right):
    return lax.dot_general(left, right, (((1,), (0,)), ((), ())), preferred_element_type=F32)


def nt(left, right):
    return lax.dot_general(left, right, (((1,), (1,)), ((), ())), preferred_element_type=F32)


def tn(left, right):
    return lax.dot_general(left, right, (((0,), (0,)), ((), ())), preferred_element_type=F32)


def gelu_pair(v):
    square = v * v
    tanh = jnp.tanh(v * (TANH_A + TANH_B * square))
    half = 0.5 + 0.5 * tanh
    value = v * half
    slope = half + value * (1.0 - tanh) * (TANH_A + 3.0 * TANH_B * square)
    return value, slope


def pad_to(count, unit):
    return -(-count // unit) * unit


WAYS = {
    (0, 0): ("xyz", "n"),
    (0, 1): ("yxz", "g"),
    (1, 0): ("myxz", "n"),
    (1, 1): ("mzxy", "g"),
    (2, 0): ("xyz", "n"),
    (2, 1): ("xyz", "g"),
}
PLAN = {
    ("O", 0, 1): ((0, 0), (0, 1)),
    ("M", 1, 1): ((0, 1), (1, 0)),
    ("M", 2, 1): ((1, 1),),
    ("O", 1): ((0, 1),),
    ("O", 2, 0): ((1, 1), (1, 0), (2, 0), (0, 1), (0, 0), (1, 1)),
    ("O", 2, 1): ((2, 0), (1, 0), (0, 1)),
    ("rows",): ((1, 1),),
    ("residual",): ((2, 1), (2, 0)),
    ("outputs",): ("mixed", (2, 0)),
    ("own", 0): ((0, 0), (2, 0), (2, 1), (0, 0), (1, 0)),
    ("own", 1): ((1, 1), (0, 0)),
    ("own", 2): ((1, 0), (2, 0)),
    ("other", 1): ((1, 1), (0, 1), (1, 0), (0, 0), "small", (2, 0)),
    ("token other",): ((2, 1), (1, 0), (1, 1), "small", (2, 1), (0, 1)),
    ("norm",): ((0, 0), (1, 0), "small", (1, 1), (2, 1), (2, 1), (0, 1), (0, 0), (1, 1), "small", (1, 0), "small"),
    ("end",): ((2, 1), (2, 0)),
}


class Sizes:
    def __init__(self, mesh_shape, patches, chan_up, token_up):
        self.dp = mesh_shape["dp"]
        self.hid = mesh_shape["hid"]
        self.xs = self.hid // 2
        self.images, self.s, self.l = patches
        self.ps = pad_to(self.s + 1, 16)
        self.wide = pad_to(self.ps, 128)
        self.d = 2 * self.l
        self.own = self.images // 2
        self.f = chan_up[1]
        self.ds = token_up[1]
        self.levels = self.dp.bit_length() - 1
        third = self.f // 3
        self.fetches = ((0, third), (third, 2 * third)) if self.f % 768 == 0 else ((0, self.f),)
        self.parts = tuple((n, third) for n in range(0, self.f, third)) if self.f % 768 == 0 else self.fetches
        self.units = [(part, kind) for part in range(len(self.parts)) for kind in range(2)]
        self.ways = {unit: ("xyz", "n") for unit in self.units}
        self.plan = {("O",) + unit: (unit,) for unit in self.units}
        if (self.xs, len(self.parts), self.levels) == (2, 3, 2):
            self.ways, self.plan = WAYS, PLAN
        self.chan_first = [unit for unit in self.units if self.ways[unit][0] in ("yxz", "myxz")]
        self.dp_first = [unit for unit in self.units if self.ways[unit][0] in ("zxy", "mzxy")]
        self.plane = 2 * self.hid
        self.blocks = -(-self.f // self.l)
        self.vec_wide = max(self.f, self.l)
        groups = 3 + self.hid * self.blocks
        self.vec_row = 2 * self.ps
        self.small = pad_to(self.vec_row + 8 * groups, 64 * self.xs)
        self.groups = (self.small - self.vec_row) // 8
        self.piece = self.small // (4 * self.xs)
        assert mesh_shape["chan"] == 2 and self.hid % 2 == 0 and self.images % 2 == 0 and self.images <= 8
        assert 1 << self.levels == self.dp and self.f % self.l == 0 and self.ds == self.l


def kernel(o, *refs):
    names = iter(refs)

    def get(count):
        return [next(names) for _ in range(count)]

    P_ = len(o.parts)
    live_hbm, patches_ref, cot_ref, tup_hbm, tdn_hbm, chan_up_ref, chan_down_ref = get(7)
    vector_hbm = get(8)
    mixed_out, grad_out, small_hbm = get(3)
    up_hbm, dn_hbm = get(P_), get(P_)
    vector_v = get(8)
    live_ref, tup_ref, tdn_ref, vec_ref, small_out = get(5)
    fin_up, fin_dn = get(P_), get(P_)
    pat, cot, cot_in, stats, stats_in, means, means2, up_s, ut_s, dn_s, dt_s, tdb_s = get(12)
    tin, th, tslope, msend, mrecv, rows_m, rows_n, inv2, vec_in = get(9)
    xs_all, gs_all, w_up, w_dn, w_b, hid_s, pg_s, out_own, ng_own, stage, ng_in, out_in = get(12)
    blow, gacc, vecs, small_send, small_c, small_p, small_in, small_z = get(8)
    gm, gb, rx, yb, ry = get(P_), get(P_), get(P_), get(P_), get(P_)
    zb, rz = dict(zip(o.units, get(2 * P_))), dict(zip(o.units, get(2 * P_)))
    ryo = {unit: next(names) for unit in o.chan_first}
    rzo = {unit: next(names) for unit in o.dp_first}
    loc_sem, send_sem, recv_sem = get(3)

    z = lax.axis_index("dp")
    y = lax.axis_index("chan")
    h = lax.axis_index("hid")
    c = h % 2
    x = h // 2
    S, PS, L, OWN, IM, X, F, N = o.s, o.ps, o.l, o.own, o.images, o.xs, o.f, o.dp
    width = float(o.d)
    here = y * o.hid + h
    bit = z % 2

    def dev(zz=None, yy=None, xx=None, cc=None):
        zz = z if zz is None else zz
        yy = y if yy is None else yy
        xx = x if xx is None else xx
        cc = c if cc is None else cc
        return (zz, yy, xx * 2 + cc)

    partner = dev(yy=1 - y)
    sibling = dev(cc=1 - c)
    z_pair = dev(zz=z + 1 - 2 * bit)
    counter = [0]

    def take(count=1):
        base = counter[0]
        counter[0] += count
        return base

    def remote(src, dst, device, index=None):
        index = take() if index is None else index
        return pltpu.make_async_remote_copy(
            src_ref=src, dst_ref=dst, send_sem=send_sem.at[index], recv_sem=recv_sem.at[index],
            device_id=device, device_id_type=MESH,
        )

    def send(src, dst, device):
        copy = remote(src, dst, device)
        copy.start()
        return copy

    barrier = pltpu.get_barrier_semaphore()
    for step in range(1, o.plane):
        there = (here + step) % o.plane
        pl.semaphore_signal(barrier, inc=1, device_id=(z, there // o.hid, there % o.hid), device_id_type=MESH)
    for step in range(1, N):
        pl.semaphore_signal(barrier, inc=1, device_id=((z + step) % N, y, h), device_id_type=MESH)

    loads = []

    def load(src, dst):
        copy = pltpu.make_async_copy(src, dst, loc_sem.at[len(loads)])
        loads.append(copy)
        copy.start()
        return copy

    stores = []

    def store(src, dst):
        copy = pltpu.make_async_copy(src, dst, loc_sem.at[24 + len(stores)])
        copy.start()
        stores.append(copy)

    load_vectors = [load(src, dst) for src, dst in zip(vector_hbm, vector_v)]
    load_live = load(live_hbm, live_ref)
    load_token = [load(tup_hbm, tup_ref), load(tdn_hbm, tdn_ref)]
    load_pat = load(patches_ref, pat)
    load_cot = load(cot_ref.at[pl.ds(y * OWN, OWN)], cot)
    load_up0 = load(chan_up_ref.at[pl.ds(pl.multiple_of(y * L, L), L)], w_up.at[0, pl.ds(0, L)])
    load_up1 = load(chan_up_ref.at[pl.ds(pl.multiple_of((1 - y) * L, L), L)], w_up.at[0, pl.ds(L, L)])
    load_dn = load(chan_down_ref, w_dn.at[0, :, pl.ds(0, L)])

    pad = PS - S
    pad_row = lax.broadcasted_iota(jnp.int32, (pad, L), 0)
    one_row = jnp.where(pad_row == 0, 1.0, 0.0).astype(BF)
    for j in range(IM):
        tin[j, S:PS, :] = one_row
    for i in range(OWN):
        xs_all[c, i, S:PS, :] = jnp.zeros((pad, o.d), BF)
        gs_all[c, i, S:PS, :] = jnp.zeros((pad, o.d), BF)
        rows_n[i, S:PS, :] = jnp.zeros((pad, o.d), F32)
        rows_m[i, S:PS, :] = jnp.zeros((pad, o.d), BF)
        inv2[i, S:PS, :] = jnp.zeros((pad, 1), F32)
        msend[i, S:PS, :] = jnp.zeros((pad, L), BF)
    vecs[...] = jnp.zeros(vecs.shape, F32)
    gacc[...] = jnp.zeros(gacc.shape, F32)
    vec_ref[...] = jnp.zeros(vec_ref.shape, F32)
    for n, copy in enumerate(load_vectors):
        copy.wait()
        count = vector_v[n].shape[0]
        vec_ref[n:n + 1, :count] = vector_v[n][...].astype(F32).reshape(1, count)
    for copy in load_token:
        copy.wait()
    w_b[0, 0:1, :] = vec_ref[7:8, :]
    up_bias, down_bias_row = vec_ref[5:6, :L], vec_ref[6:7, :L]
    last = jnp.zeros((o.wide - S - 1, L), F32)
    up_full = jnp.concatenate([tup_ref[...].astype(F32), up_bias, last], 0)
    up_s[...] = up_full[:PS].astype(BF)
    ut_s[...] = up_full.T[:, :PS].astype(BF)
    dn_full = jnp.concatenate([tdn_ref[...].astype(F32), jnp.zeros((o.wide - S, L), F32)], 0)
    dn_s[...] = dn_full.T[:, :PS].astype(BF)
    dt_s[...] = dn_full[:PS].astype(BF)
    tdb_s[...] = jnp.concatenate([down_bias_row, jnp.zeros((127, L), F32)], 0).T[:PS]

    lane = lax.broadcasted_iota(jnp.int32, (S, 128), 1)
    load_pat.wait()

    def note(table, j, first, second):
        table = jnp.where(lane == j, first, table)
        return jnp.where(lane == j + 8, second, table)

    def across(table):
        rest = jnp.zeros((o.wide - S, 128), F32)
        return jnp.concatenate([table, rest], 0).T[:16]

    def along(table):
        return jnp.concatenate([table, jnp.zeros((112, o.wide), F32)], 0).T

    def sums_of(j, table):
        v = pat[j].astype(F32)
        return note(table, j, jnp.sum(v, -1, keepdims=True), jnp.sum(v * v, -1, keepdims=True))

    stats[0] = across(lax.fori_loop(0, IM, sums_of, jnp.zeros((S, 128), F32)))

    pl.semaphore_wait(barrier, o.plane - 1 + N - 1)

    copy_stats = send(stats.at[0], stats_in.at[0], partner)
    copy_vec = send(vec_ref, vec_in, partner)
    near = pl.ds(bit * L, L)
    near_from = pl.ds(pl.multiple_of(((y + bit) % 2) * L, L), L)
    copy_b = {step: send(w_b.at[0], w_b.at[step], dev(xx=(x + step) % X)) for step in range(1, X)}
    copy_w = {}
    copy_f = {}

    def weight_spans(step, part):
        start, size = o.fetches[part]
        cols = pl.ds(start, size)
        rows_dn = pl.ds(pl.multiple_of(start + bit * (size // 2), 16), size // 2)
        rows_own = pl.ds(start, size) if part else rows_dn
        return (
            (chan_up_ref.at[near_from, cols], w_up.at[step, near, cols], y),
            (chan_down_ref.at[rows_own], w_dn.at[step, rows_own, pl.ds(0, L)], y),
            (chan_down_ref.at[rows_dn], w_dn.at[step, rows_dn, pl.ds(L, L)], 1 - y),
        )

    def fetch(part, which):
        for step in range(1, X):
            for n in which if part < len(o.fetches) else ():
                src, dst, yy = weight_spans(step, part)[n]
                copy_w[step, part, n] = send(src, dst, dev(xx=(x + step) % X, yy=yy))

    def hand_on(part, which):
        for step in range(1, X):
            for n in which if part < len(o.fetches) else ():
                dst = weight_spans(step, part)[n][1]
                if part and n == 1:
                    copy_f[step, part, n] = copy_w[step, part, n]
                else:
                    copy_w[step, part, n].wait()
                    copy_f[step, part, n] = send(dst, dst, z_pair)

    quarter = F // 4
    bit2 = (z // 2) % 2
    z_far = dev(zz=z + 2 - 4 * bit2)

    def dn2_span(first, count):
        return pl.ds(pl.multiple_of(first * quarter, 16), count * quarter)

    dn2_mine = dn2_span(bit * 2 + bit2, 1)
    dn2_half = dn2_span(bit * 2, 2)
    copy_dn2 = [send(chan_down_ref.at[dn2_mine], w_dn.at[0, dn2_mine, pl.ds(L, L)], partner)]

    def dn2_on(span, peer):
        copy_dn2[-1].wait()
        ref = w_dn.at[0, span, pl.ds(L, L)]
        copy_dn2.append(send(ref, ref, peer))

    fetch(0, (0,))
    copy_cot = send(cot_ref.at[pl.ds((1 - y) * OWN, OWN)], cot_in, partner)
    fetch(0, (1, 2))

    copy_stats.wait()
    total = (stats[0] + stats_in[0]) * (1.0 / width)
    mean, square = total[:8], total[8:]
    means[...] = along(jnp.concatenate([mean, lax.rsqrt(square - mean * mean + EPS)], 0))
    fetch(1, (0,))

    def column(table, j):
        return jnp.sum(jnp.where(lane == j, table, 0.0), -1, keepdims=True)

    first_gain = vec_ref[0:1, :L]
    first_shift = vec_ref[1:2, :L]

    def first_norm(j):
        table = means[:S, :]
        inv_one = column(table, j + 8)
        return (pat[j].astype(F32) - column(table, j)) * inv_one, inv_one

    def token_forward(j):
        normed, _ = first_norm(j)
        tin[j, :S, :] = (normed * first_gain + first_shift).astype(BF)
        value, slope = gelu_pair(nn(ut_s[...], tin[j]))
        th[j] = value.astype(BF)
        tslope[j] = slope.astype(BF)
        back = nn(dt_s[...], th[j])
        return pat[j].astype(F32) + back[:S] + tdb_s[:S, 0:1]

    mixed_sems = take(OWN)

    def copy_mixed(i):
        return remote(msend.at[i], mrecv.at[i], partner, mixed_sems + i)

    @pl.loop(0, OWN)
    def _(i):
        msend[i, :S, :] = token_forward((1 - y) * OWN + i).astype(BF)
        copy_mixed(i).start()

    @pl.loop(0, OWN)
    def _(i):
        rows_n[i, :S, :L] = token_forward(y * OWN + i)

    dn2_on(dn2_mine, z_far)
    hand_on(0, (0,))
    fetch(1, (1,))
    hand_on(0, (1, 2))
    dn2_on(dn2_half, z_pair)
    load_cot.wait()
    copy_cot.wait()
    load_live.wait()
    live = live_ref[0]

    def keep_of(j):
        return jnp.where(j < live, 1.0, 0.0).astype(F32)

    @pl.loop(0, OWN)
    def _(i):
        keep = keep_of(y * OWN + i)
        gs_all[c, i, :S, :L] = (cot[i].astype(F32) * keep).astype(BF)
        gs_all[c, i, :S, L:] = (cot_in[i].astype(F32) * keep).astype(BF)

    copy_gs = send(gs_all.at[c], gs_all.at[c], sibling)
    hand_on(1, (0,))

    copy_vec.wait()
    both = [jnp.concatenate([vec_ref[n:n + 1, :L], vec_in[n:n + 1, :L]], axis=1) for n in range(2, 5)]
    second_gain, second_shift, down_bias = both
    row_sems = take(OWN)

    def copy_rows(i):
        return remote(xs_all.at[c, i], xs_all.at[c, i], sibling, row_sems + i)

    @pl.loop(0, OWN)
    def _(i):
        copy_mixed(i).wait()
        rows_n[i, :S, L:] = mrecv[i, :S, :].astype(F32)
        v = rows_n[i, :S, :]
        mean = jnp.sum(v, -1, keepdims=True) * (1.0 / width)
        spread = jnp.sum(v * v, -1, keepdims=True) * (1.0 / width) - mean * mean
        inv_two = lax.rsqrt(spread + EPS)
        normed = (v - mean) * inv_two
        rows_m[i, :S, :] = v.astype(BF)
        inv2[i, :S, :] = inv_two
        rows_n[i, :S, :] = normed
        xs_all[c, i, :S, :] = (normed * second_gain + second_shift).astype(BF)
        copy_rows(i).start()

    fetch(1, (2,))
    hand_on(1, (1,))
    load_up0.wait()
    load_up1.wait()
    load_dn.wait()
    copy_gs.wait()

    @pl.loop(0, OWN)
    def _(i):
        copy_rows(i).wait()

    def levels():
        start, count, used = 0, N, 0
        for level in range(o.levels):
            side_bit = (z // (1 << level)) % 2
            peer = dev(zz=z + (1 - 2 * side_bit) * (1 << level))
            count //= 2
            yield start + side_bit * count, start + (1 - side_bit) * count, count, used, peer
            start = start + side_bit * count
            used += count

    def my_segment():
        return list(levels())[-1][0]

    def add(part, kind, half, span, *terms):
        mine = gm[part][kind, half, span]
        for term in terms:
            mine = mine + term.astype(F32)
        gm[part][kind, half, span] = mine

    everything = pl.ds(0, N)
    low, high = pl.ds(0, N // 2), pl.ds(N // 2, N // 2)

    def finals(part, kind):
        if kind == 0:
            return [fin_up[part].at[0], fin_up[part].at[1]]
        return [fin_dn[part]]

    def reduce_rec(part, kind, halves):
        out, land = zb[part, kind], rz[part, kind]
        for keep_at, send_at, count, used, peer in levels():
            span = pl.ds(used, count)
            copies = []
            for half in range(halves):
                out[half, span] = gm[part][kind, half, pl.ds(send_at, count)].astype(BF)
                copies.append(send(out.at[half, span], land.at[half, span], peer))
            yield
            for half in range(halves):
                copies[half].wait()
                add(part, kind, half, pl.ds(keep_at, count), land[half, span])

    def gather_rec(part, kind):
        own = pl.ds(my_segment(), 1)
        done = finals(part, kind)
        early = kind == 0 and o.ways[part, kind][1] == "g"
        done[0][own] = gm[part][kind, 0, own].astype(BF)
        if early:
            copy = send(done[0].at[own], done[1].at[own], partner)
            yield
            copy.wait()
        for keep_at, _, count, _, peer in reversed(list(levels())):
            span = pl.ds(keep_at, count)
            copies = [send(ref.at[span], ref.at[span], peer) for ref in done[:1 + early]]
            yield
            for copy in copies:
                copy.wait()
        if kind == 0 and not early:
            copy = send(done[0], done[1], partner)
            yield
            copy.wait()

    def owner(n):
        return dev(xx=(x + X - 1 - n) % X)

    def start_x(part, kind):
        return [send(gb[part].at[n, kind], rx[part].at[n, kind], owner(n)) for n in range(X - 1)]

    def send_y(part, kind, span):
        yb[part][kind, span] = gm[part][kind, 1, span].astype(BF)
        return send(yb[part].at[kind, span], ry[part].at[kind, span], partner)

    def wait_all(copies):
        for copy in copies:
            copy.wait()

    def add_x(part, kind, half, span):
        add(part, kind, half, span, *[rx[part][n, kind, half, span] for n in range(X - 1)])

    def chunk_xyz(part, kind):
        copies = start_x(part, kind)
        yield
        wait_all(copies)
        add_x(part, kind, 1, everything)
        copy = send_y(part, kind, everything)
        add_x(part, kind, 0, everything)
        yield
        copy.wait()
        add(part, kind, 0, everything, ry[part][kind])
        yield from reduce_rec(part, kind, 1)
        yield from gather_rec(part, kind)

    def chunk_xzy(part, kind):
        copies = start_x(part, kind)
        yield
        wait_all(copies)
        add_x(part, kind, 1, everything)
        add_x(part, kind, 0, everything)
        yield from reduce_rec(part, kind, 2)
        own = pl.ds(my_segment(), 1)
        copy = send_y(part, kind, own)
        yield
        copy.wait()
        add(part, kind, 0, own, ry[part][kind, own])
        yield from gather_rec(part, kind)

    def start_yo(part, kind):
        return [send(gb[part].at[n, kind, 1], ryo[part, kind].at[n], partner) for n in range(X - 1)]

    def pass_yo(part, kind, copies):
        wait_all(copies)
        for n in range(X - 1):
            mine = gb[part][n, kind, 0].astype(F32) + ryo[part, kind][n].astype(F32)
            gb[part][n, kind, 0] = mine.astype(BF)
        return [send(gb[part].at[n, kind, 0], rx[part].at[n, kind, 0], owner(n)) for n in range(X - 1)]

    def end_yx(part, kind, copies, copy):
        copy.wait()
        wait_all(copies)
        add(part, kind, 0, everything, ry[part][kind], *[rx[part][n, kind, 0] for n in range(X - 1)])
        yield from reduce_rec(part, kind, 1)
        yield from gather_rec(part, kind)

    def chunk_yxz(part, kind):
        copies = start_yo(part, kind)
        yield
        copies = pass_yo(part, kind, copies)
        yield
        copy = send_y(part, kind, everything)
        yield
        yield from end_yx(part, kind, copies, copy)

    def chunk_myxz(part, kind):
        copy = send_y(part, kind, everything)
        yield
        copies = start_yo(part, kind)
        yield
        copies = pass_yo(part, kind, copies)
        yield
        yield from end_yx(part, kind, copies, copy)

    def reduce_others(part, kind):
        land = rzo[part, kind]
        for keep_at, send_at, count, used, peer in levels():
            copies = {}
            span = pl.ds(used, count)
            for n in range(X - 1):
                for half in range(2):
                    src = gb[part].at[n, kind, half, pl.ds(send_at, count)]
                    copies[n, half] = send(src, land.at[n, half, span], peer)
            yield
            for n in range(X - 1):
                for half in range(2):
                    copies[n, half].wait()
                    keep = pl.ds(keep_at, count)
                    mine = gb[part][n, kind, half, keep].astype(F32) + land[n, half, span].astype(F32)
                    gb[part][n, kind, half, keep] = mine.astype(BF)

    def segment_x(part, kind):
        own = pl.ds(my_segment(), 1)
        return [send(gb[part].at[n, kind, :, own], rx[part].at[n, kind, :, own], owner(n)) for n in range(X - 1)]

    def end_zx(part, kind, copies):
        own = pl.ds(my_segment(), 1)
        wait_all(copies)
        add_x(part, kind, 1, own)
        copy = send_y(part, kind, own)
        add_x(part, kind, 0, own)
        yield
        copy.wait()
        add(part, kind, 0, own, ry[part][kind, own])
        yield from gather_rec(part, kind)

    def chunk_zxy(part, kind):
        yield from reduce_others(part, kind)
        copies = segment_x(part, kind)
        yield
        yield from reduce_rec(part, kind, 2)
        yield from end_zx(part, kind, copies)

    def chunk_mzxy(part, kind):
        yield from reduce_rec(part, kind, 2)
        yield from reduce_others(part, kind)
        copies = segment_x(part, kind)
        yield
        yield from end_zx(part, kind, copies)

    chunk = {
        "xyz": chunk_xyz, "xzy": chunk_xzy, "yxz": chunk_yxz, "myxz": chunk_myxz, "zxy": chunk_zxy, "mzxy": chunk_mzxy
    }
    pipes = {unit: chunk[o.ways[unit][0]](*unit) for unit in o.units}

    def step_of(name):
        if name in pipes:
            try:
                next(pipes[name])
            except StopIteration:
                del pipes[name]
                if name == "small":
                    store(small_out, small_hbm)
                elif name != "mixed":
                    part, kind = name
                    store(*((fin_up[part], up_hbm[part]), (fin_dn[part], dn_hbm[part]))[kind])

    def at(*point):
        for name in o.plan.get(point, ()):
            step_of(name)

    rows = OWN * PS

    def inner(step, start, size):
        cols = pl.ds(start, size)

        def side(cc, sums):
            pre = nn(xs_all[cc].reshape(rows, o.d), w_up[step, :, cols]) + w_b[step, 0:1, cols]
            value, slope = gelu_pair(pre)
            hid_s[step, cc, :, cols] = value.astype(BF)
            grad = (nt(gs_all[cc].reshape(rows, o.d), w_dn[step, cols, :]) * slope).astype(BF)
            pg_s[step, cc, :, cols] = grad
            return sums + jnp.sum(grad.astype(F32), 0, keepdims=True)

        sums = lax.fori_loop(0, 2, side, jnp.zeros((1, size), F32))
        group = 3 + ((x + X - step) % X * 2 + c) * o.blocks
        for n in range(start, start + size, 128):
            block, lanes = n // L, n % L
            vecs[group + block, 0:1, lanes:lanes + 128] = sums[:, n - start:n - start + 128]

    def weight_grad(step, part, kind):
        start, size = o.parts[part]
        cols = pl.ds(start, size)
        left, right = (pg_s, xs_all) if kind == 0 else (hid_s, gs_all)
        grad = tn(left[step, :, :, cols].reshape(2 * rows, size), right[...].reshape(2 * rows, o.d))
        grad = grad.reshape(N, size // N, o.d)
        for half in range(2):
            block = grad[:, :, half * L:(half + 1) * L]
            if step:
                gb[part][step - 1, kind, half] = block.astype(BF)
            else:
                gm[part][kind, half] = block

    def other_slots(group):
        start, size = o.fetches[group]
        for step in range(1, X):
            if group == 0:
                copy_b[step].wait()
            for n in range(3):
                copy_f[step, group, n].wait()
            inner(step, start, size)
        at("O", group)
        for part in range(P_):
            if start <= o.parts[part][0] < start + size:
                for kind in range(2):
                    for step in range(1, X):
                        weight_grad(step, part, kind)
                    at("O", part, kind)

    other_slots(0)
    hand_on(1, (2,))
    copy_dn2[-1].wait()
    inner(0, 0, F)
    at("M")
    for part in range(P_):
        for kind in range(2):
            weight_grad(0, part, kind)
            at("M", part, kind)
    for group in range(1, len(o.fetches)):
        other_slots(group)
    at("O")

    def row_sums(kind, cc):
        left, right, dot = ((pg_s, w_up, nt), (hid_s, w_dn, nn))[kind]
        total = dot(left[0, cc], right[0])
        for step in range(1, X):
            total = total + dot(left[step, cc], right[step])
        return total

    stage[0] = row_sums(0, 1 - c).astype(BF)
    copy_ng = send(stage.at[0], ng_in, sibling)
    mine = row_sums(0, c)
    ng_own[0] = mine[:, :L]
    ng_own[1] = mine[:, L:]
    at("rows")

    res_sems = take(OWN)

    def copy_res(i):
        return remote(mrecv.at[i], blow.at[y * OWN + i], partner, res_sems + i)

    copy_ng.wait()

    def residual(i, sums):
        block = pl.ds(pl.multiple_of(i * PS, 16), PS)
        ng = jnp.concatenate([ng_own[0, block, :], ng_own[1, block, :]], 1) + ng_in[block, :].astype(F32)
        normed = rows_n[i]
        back = gs_all[c, i].astype(F32)
        sums = (
            sums[0] + jnp.sum(ng * normed, 0, keepdims=True),
            sums[1] + jnp.sum(ng, 0, keepdims=True),
            sums[2] + jnp.sum(back, 0, keepdims=True),
        )
        q = ng * second_gain
        m1 = jnp.sum(q, -1, keepdims=True) * (1.0 / width)
        m2 = jnp.sum(q * normed, -1, keepdims=True) * (1.0 / width)
        res = (back + inv2[i] * (q - m1 - normed * m2)).astype(BF)
        mrecv[i] = res[:, L:]
        copy_res(i).start()
        blow[y * OWN + i] = res[:, :L]
        return sums

    zero = jnp.zeros((1, o.d), F32)
    sums = lax.fori_loop(0, OWN, residual, (zero, zero, zero))
    for n in range(3):
        vecs[0, 1 + 2 * n:2 + 2 * n, :] = jnp.where(y == 0, sums[n][:, :L], sums[n][:, L:])
        vecs[0, 2 + 2 * n:3 + 2 * n, :] = jnp.where(y == 0, sums[n][:, L:], sums[n][:, :L])
    at("residual")

    stage[1] = row_sums(1, 1 - c).astype(BF)
    copy_out = send(stage.at[1], out_in, sibling)
    at("outputs 0")
    out_own[...] = row_sums(1, c)

    mixed_sems2 = take(OWN)

    def copy_mo(i):
        return remote(msend.at[i], mixed_out.at[y * OWN + i], partner, mixed_sems2 + i)

    def output_rows():
        copy_out.wait()

        @pl.loop(0, OWN)
        def _(i):
            block = pl.ds(pl.multiple_of(i * PS, 16), PS)
            branch = out_own[block, :] + out_in[block, :].astype(F32) + down_bias
            result = (keep_of(y * OWN + i) * (rows_m[i].astype(F32) + branch)).astype(BF)
            msend[i] = result[:, L:]
            copy_mo(i).start()
            xs_all[c, i, :, :L] = result[:, :L]

        store(xs_all.at[c, :, :, pl.ds(0, L)], mixed_out.at[pl.ds(y * OWN, OWN)])
        yield

    pipes["mixed"] = output_rows()
    at("outputs")

    ones = jnp.ones((16, L), BF)

    def scaled(j):
        return j // OWN, pl.ds(pl.multiple_of(j % OWN * PS, 16), PS)

    def token_backward(j, carry):
        table, sum_gain, sum_shift, sum_bias = carry
        low_grad = blow[j]
        grad = (nn(dn_s[...], low_grad) * tslope[j].astype(F32)).astype(BF)
        gacc[0] += nt(tin[j], grad)
        gacc[1] += nt(low_grad, th[j])
        sum_bias = sum_bias + nt(ones, low_grad)
        back = nn(up_s[...], grad)
        normed, _ = first_norm(j)
        sum_gain = sum_gain + jnp.sum(back[:S] * normed, 0, keepdims=True)
        sum_shift = sum_shift + jnp.sum(back[:S], 0, keepdims=True)
        back = back * first_gain
        ng_own[scaled(j)] = back
        back = back[:S]
        table = note(table, j, jnp.sum(back, -1, keepdims=True), jnp.sum(back * normed, -1, keepdims=True))
        return table, sum_gain, sum_shift, sum_bias

    carry = (jnp.zeros((S, 128), F32), jnp.zeros((1, L), F32), jnp.zeros((1, L), F32), jnp.zeros((16, PS), F32))
    for i in range(OWN):
        carry = token_backward(y * OWN + i, carry)
        at("own", i)

    for i in range(OWN):
        copy_res(i).wait()
        carry = token_backward((1 - y) * OWN + i, carry)
        if i < OWN - 1:
            at("other", i)
    table, sum_gain, sum_shift, sum_bias = carry
    stats[1] = across(table)
    copy_stats2 = send(stats.at[1], stats_in.at[1], partner)
    vecs[0, 0:1, :PS] = sum_bias[0:1, :]
    vecs[1 + y, 0:1, :] = sum_gain
    vecs[1 + y, 1:2, :] = sum_shift

    half_small = o.small // 2
    spot = y * X + x
    chips = 2 * X

    def chip_peers():
        for step in range(1, chips):
            there = (spot + step) % chips
            yield step, there, dev(yy=there // X, xx=there % X)

    def piece(n):
        return pl.ds(pl.multiple_of(n * o.piece, 16), o.piece)

    def share(cc):
        return pl.ds(pl.multiple_of(cc * half_small, 16), half_small)

    def out_piece(n):
        return pl.ds(pl.multiple_of(c * half_small + n * o.piece, 16), o.piece)

    small_send[0:PS, :] = gacc[0]
    small_send[PS:2 * PS, :] = gacc[1]
    small_send[o.vec_row:, :] = vecs[...].reshape(8 * o.groups, L)

    def reduce_small():
        copy = send(small_send.at[share(1 - c)], small_c, sibling)
        yield
        copy.wait()
        small_p[...] = (small_send[share(c), :] + small_c[...]).astype(BF)
        copies = [send(small_p.at[piece(there)], small_in.at[n - 1], peer) for n, there, peer in chip_peers()]
        yield
        for copy in copies:
            copy.wait()
        mine = small_p[piece(spot), :].astype(F32)
        for n in range(1, chips):
            mine = mine + small_in[n - 1].astype(F32)
        small_z[z] = mine.astype(BF)
        copies = [send(small_z.at[z], small_z.at[z], dev(zz=(z + n) % N)) for n in range(1, N)]
        yield
        for copy in copies:
            copy.wait()
        mine = small_z[0].astype(F32)
        for n in range(1, N):
            mine = mine + small_z[n].astype(F32)
        small_out[out_piece(spot), :] = mine.astype(BF)
        span = small_out.at[out_piece(spot)]
        copies = [send(span, span, peer) for _, _, peer in chip_peers()]
        yield
        for copy in copies:
            copy.wait()
        span = small_out.at[share(c)]
        copy = send(span, span, sibling)
        yield
        copy.wait()

    pipes["small"] = reduce_small()
    step_of("small")
    at("token other")

    copy_stats2.wait()
    means2[...] = along((stats[1] + stats_in[1]) * (1.0 / width))

    @pl.loop(0, IM)
    def _(j):
        normed, inv_one = first_norm(j)
        grad = ng_own[scaled(j)][:S]
        grad = grad - column(means2[:S, :], j) - normed * column(means2[:S, :], j + 8)
        blow[j, :S, :] = (blow[j, :S, :].astype(F32) + inv_one * grad).astype(BF)

    store(blow, grad_out)
    at("norm")

    while pipes:
        for name in list(pipes):
            step_of(name)

    @pl.loop(0, OWN)
    def _(i):
        copy_mo(i).wait()

    for copy in stores:
        copy.wait()


def block_call(o, matrices, vectors):
    I, S, PS, L, OWN, D, X, N, F = o.images, o.s, o.ps, o.l, o.own, o.d, o.xs, o.dp, o.f
    any_spec = pl.BlockSpec(memory_space=pl.ANY)
    rows = OWN * PS
    copies = 16 + 4 * OWN + (X - 1) * (1 + 6 * len(o.parts)) + 6 * X + N
    copies += len(o.units) * ((X - 1) * (3 + 2 * o.levels) + 5 * o.levels + 8)
    segs = [size // N for _, size in o.parts]
    outs = [
        jax.ShapeDtypeStruct((I, PS, L), BF),
        jax.ShapeDtypeStruct((I, PS, L), BF),
        jax.ShapeDtypeStruct((o.small, L), BF),
    ]
    outs += [jax.ShapeDtypeStruct((2, N, seg, L), BF) for seg in segs]
    outs += [jax.ShapeDtypeStruct((N, seg, L), BF) for seg in segs]
    scratch = [(vector.shape, BF) for vector in vectors]
    scratch += [None, ((S, L), BF), ((S, L), BF), ((8, o.vec_wide), F32), ((o.small, L), BF)]
    scratch += [((2, N, seg, L), BF) for seg in segs] + [((N, seg, L), BF) for seg in segs]
    scratch += [
        ((I, S, L), BF), ((OWN, S, L), BF), ((OWN, S, L), BF),
        ((2, 16, o.wide), F32), ((2, 16, o.wide), F32),
        ((o.wide, 128), F32), ((o.wide, 128), F32),
        ((PS, L), BF), ((L, PS), BF), ((L, PS), BF), ((PS, L), BF), ((PS, 128), F32),
        ((I, PS, L), BF), ((I, o.ds, L), BF), ((I, o.ds, L), BF),
        ((OWN, PS, L), BF), ((OWN, PS, L), BF),
        ((OWN, PS, D), BF), ((OWN, PS, D), F32), ((OWN, PS, 1), F32), ((8, o.vec_wide), F32),
        ((2, OWN, PS, D), BF), ((2, OWN, PS, D), BF),
        ((X, D, F), BF), ((X, F, D), BF), ((X, 8, o.vec_wide), F32),
        ((X, 2, rows, F), BF), ((X, 2, rows, F), BF),
        ((rows, D), F32), ((2, rows, L), F32), ((2, rows, D), BF),
        ((rows, D), BF), ((rows, D), BF),
        ((I, PS, L), BF), ((2, PS, L), F32), ((o.groups, 8, L), F32),
        ((o.small, L), F32), ((o.small // 2, L), F32), ((o.small // 2, L), BF),
        ((2 * X - 1, o.piece, L), BF), ((N, o.piece, L), BF),
    ]
    blocks = [(N, seg, L) for seg in segs]
    scratch += [((2, 2) + block, F32) for block in blocks]
    scratch += [((X - 1, 2, 2) + block, BF) for block in blocks] * 2
    scratch += [((2,) + block, BF) for block in blocks] * 2
    for _ in range(2):
        for unit in o.units:
            halves = 1 if o.ways[unit][0] in ("xyz", "yxz", "myxz") else 2
            scratch.append(((halves,) + blocks[unit[0]], BF))
    scratch += [((X - 1,) + blocks[unit[0]], BF) for unit in o.chan_first]
    scratch += [((X - 1, 2) + blocks[unit[0]], BF) for unit in o.dp_first]
    return pl.pallas_call(
        functools.partial(kernel, o),
        out_shape=outs,
        in_specs=[any_spec] * (len(matrices) + len(vectors)),
        out_specs=[any_spec] * len(outs),
        scratch_shapes=[pltpu.VMEM(*entry) if entry else pltpu.SMEM((1,), jnp.int32) for entry in scratch]
        + [pltpu.SemaphoreType.DMA((40,)), pltpu.SemaphoreType.DMA((copies,)), pltpu.SemaphoreType.DMA((copies,))],
        compiler_params=pltpu.CompilerParams(
            collective_id=1, has_side_effects=True, vmem_limit_bytes=63 * 2**20
        ),
        name="mixer_block",
    )(*matrices, *vectors)


def unpack(o, *refs):
    P_ = len(o.parts)
    names = iter(refs)

    def get(count):
        return [next(names) for _ in range(count)]

    inputs, outputs = get(3 + 2 * P_), get(14)
    inputs_v, outputs_v = get(3 + 2 * P_), get(14)
    in_sem, out_sem = get(2)
    S, PS, L = o.s, o.ps, o.l
    y = lax.axis_index("chan")
    h = lax.axis_index("hid")
    loads = [pltpu.make_async_copy(src, dst, in_sem.at[n]) for n, (src, dst) in enumerate(zip(inputs, inputs_v))]
    stores = [pltpu.make_async_copy(src, dst, out_sem.at[n]) for n, (src, dst) in enumerate(zip(outputs_v, outputs))]
    order = list(range(3, 3 + 2 * P_)) + [0, 1, 2]
    for n in order:
        loads[n].start()
    mixed_in, grad_in, small_in = inputs_v[:3]
    fin_up, fin_dn = inputs_v[3:3 + P_], inputs_v[3 + P_:]
    mixed, grad, fg, fs, tu, tub, td, tdb, sg, ss, cu, cub, cd, cdb = outputs_v
    for part, (start, size) in enumerate(o.parts):
        loads[3 + part].wait()
        for half in range(2):
            block = fin_up[part][half].astype(F32).reshape(size, L).T
            cu[pl.ds(pl.multiple_of((y + half) % 2 * L, L), L), start:start + size] = block
    stores[10].start()
    for part, (start, size) in enumerate(o.parts):
        loads[3 + P_ + part].wait()
        cd[start:start + size, :] = fin_dn[part][...].astype(F32).reshape(size, L)
    stores[12].start()
    loads[0].wait()
    mixed[...] = mixed_in[:, :S]
    stores[0].start()
    loads[1].wait()
    grad[...] = grad_in[:, :S]
    stores[1].start()
    loads[2].wait()
    small = small_in[...].astype(F32)
    tu[...] = small[:S]
    tub[...] = small[S:S + 1].reshape(L)
    td[...] = small[PS:PS + S]
    groups = small[o.vec_row:].reshape(o.groups, 8, L)
    tdb[...] = groups[0, 0:1, :S].reshape(S)
    for n, ref in enumerate((sg, ss, cdb)):
        ref[...] = jnp.where(y == 0, groups[0, 1 + 2 * n:2 + 2 * n], groups[0, 2 + 2 * n:3 + 2 * n]).reshape(L)
    for n, ref in enumerate((fg, fs)):
        ref[...] = jnp.where(y == 0, groups[1, n:n + 1], groups[2, n:n + 1]).reshape(L)
    totals = []
    for n in range(o.blocks):
        total = jnp.zeros((1, L), F32)
        for k in range(o.hid):
            total = jnp.where(h == k, groups[3 + k * o.blocks + n, 0:1], total)
        totals.append(total)
    cub[...] = jnp.concatenate(totals, 1).reshape(o.f)
    for n in (2, 3, 4, 5, 6, 7, 8, 9, 11, 13):
        stores[n].start()
    for copy in stores:
        copy.wait()


def body(
    o,
    patches,
    cotangent,
    live_images,
    first_gain,
    first_shift,
    token_up,
    token_up_bias,
    token_down,
    token_down_bias,
    second_gain,
    second_shift,
    chan_up,
    chan_up_bias,
    chan_down,
    chan_down_bias,
):
    S, L, D, F = o.s, o.l, o.d, o.f
    matrices = [live_images, patches, cotangent, token_up, token_down.T, chan_up, chan_down]
    vectors = [first_gain, first_shift, second_gain, second_shift, chan_down_bias, token_up_bias, token_down_bias]
    results = block_call(o, matrices, vectors + [chan_up_bias])
    any_spec = pl.BlockSpec(memory_space=pl.ANY)
    shapes = [
        (patches.shape, BF), (patches.shape, BF), ((L,), F32), ((L,), F32), ((S, L), F32), ((L,), F32),
        ((S, L), F32), ((S,), F32), ((L,), F32), ((L,), F32), ((D, F), F32), ((F,), F32), ((F, L), F32),
        ((L,), F32),
    ]
    outs = pl.pallas_call(
        functools.partial(unpack, o),
        out_shape=[jax.ShapeDtypeStruct(shape, kind) for shape, kind in shapes],
        in_specs=[any_spec] * len(results),
        out_specs=[any_spec] * len(shapes),
        scratch_shapes=[pltpu.VMEM(result.shape, BF) for result in results]
        + [pltpu.VMEM(shape, kind) for shape, kind in shapes]
        + [pltpu.SemaphoreType.DMA((len(results),)), pltpu.SemaphoreType.DMA((len(shapes),))],
        compiler_params=pltpu.CompilerParams(vmem_limit_bytes=63 * 2**20),
        name="unpack",
    )(*results)
    return tuple(out.T if n == 6 else out for n, out in enumerate(outs))


def solution(mesh):
    in_specs = (
        P(("dp", "hid"), None, "chan"),
        P(("dp", "hid"), None, "chan"),
        P(("dp", "hid")),
        P("chan"),
        P("chan"),
        P(),
        P(),
        P(),
        P(),
        P("chan"),
        P("chan"),
        P(None, "hid"),
        P("hid"),
        P("hid", "chan"),
        P("chan"),
    )
    out_specs = (
        P(("dp", "hid"), None, "chan"),
        P(("dp", "hid"), None, "chan"),
        P("chan"),
        P("chan"),
        P(),
        P(),
        P(),
        P(),
        P("chan"),
        P("chan"),
        P(None, "hid"),
        P("hid"),
        P("hid", "chan"),
        P("chan"),
    )

    def whole(*args):
        shape = dict(mesh.shape)
        patches, token_up, chan_up = args[0].shape, args[5].shape, args[11].shape
        local = (patches[0] // (shape["dp"] * shape["hid"]), patches[1], patches[2] // shape["chan"])
        o = Sizes(shape, local, (chan_up[0], chan_up[1] // shape["hid"]), token_up)
        mapped = jax.shard_map(
            functools.partial(body, o), mesh=mesh, in_specs=in_specs, out_specs=out_specs, check_vma=False
        )
        return mapped(*args)

    return whole
```

time: 162 us -> 126 us (0.78); the launches traced: 160 us -> 126 us
  local copies, waits for them, and re-layouts: 17.2 us -> 0 us
  Pallas kernels: 138 us -> 125 us
  other arithmetic: 2.86 us -> 0 us
    pallas_call x1 -> x2, Pallas kernels: 138 us -> 125 us  [the longest x1 120 us: block_call(): pl.pallas_call(functools.partial(kernel, o), out_shape=outs, in_specs=[an...]
    slice x6 -> x0, local copies, waits for them, and re-layouts: 4.63 us -> none  [the longest x1 2.28 us: body(): mixed[:, :S]]
    pad x3 -> x0, local copies, waits for them, and re-layouts: 2.99 us -> none  [the longest x1 1.59 us: body(): up = jnp.pad(token_up, ((0, rest), (0, 0)))]
    unnamed x27 -> x0, local copies, waits for them, and re-layouts: 2.83 us -> none
    broadcast_in_dim x4 -> x0, local copies, waits for them, and re-layouts: 2.18 us -> none  [the longest x1 0.79 us: body(): token_up_bias[None]]
    convert_element_type x4 -> x0, other arithmetic: 2.08 us -> none  [the longest x1 1.15 us: body(): gdn.reshape(o.f, L).astype(F32)]
    convert_element_type x1 -> x0, local copies, waits for them, and re-layouts: 1.82 us -> none  [body(): gup.reshape(o.chunks, 2, L, L).transpose(1, 2, 0, 3).reshape(o.d, o.f)]
where the time goes in v3:
time: 126 us
  Pallas kernels  125 us (99%)
  between operations  1.48 us (1%)
    pallas_call x1, Pallas kernels, block_call(): pl.pallas_call(functools.partial(kernel, o), out_shape=outs, in_specs=[an...  120 us
    pallas_call x1, Pallas kernels, body(): pl.pallas_call(functools.partial(unpack, o), out_shape=[jax.ShapeDtypeStr...  4.3 us

profile of v3, /device:TPU:0, one launch (start us, length us, event | category | flops | bytes accessed | tf_op | source)
XLA Modules:
  0.0 126.2 jit_solution(1670684029190115787)
XLA Ops:
  1.3 120.4 %mixer_block.1 = (bf16[6,208,384]{2,1,0:T(8,128)(2,1)}, bf16[6,208,384]{2,1,0:T(8,128)(2,1)}, bf16[512,384]{1,0:T(8,128)(2,1)}, bf16[2,4,64,384]{3,2,1,0:T(8,128...) custom-call(s32[1]{0:T(128)S(6)} %copy.29.refs_0_, ...), custom_call_target="tpu_custom_call" | custom-call | tf_op jit(solution)/shard_map/mixer_block/pallas_call | solution.py:912
  121.7 4.3 %unpack.1 = (bf16[6,196,384]{2,1,0:T(8,128)(2,1)}, bf16[6,196,384]{2,1,0:T(8,128)(2,1)}, f32[384]{0:T(512)}, f32[384]{0:T(512)}, f32[196,384]{1,0:T(8,128)}, /*i...) custom-call(bf16[6,208,384]{2,1,0:T(8,128)(2,1)} %get-tuple-element., ...), custom_call_target="tpu_custom_call" | custom-call | tf_op jit(solution)/shard_map/unpack/pallas_call | solution.py:1015

commit v4 on v3

--- a/solution.py
+++ b/solution.py
@@ -41,30 +41,33 @@
 
 
 WAYS = {
-    (0, 0): ("xyz", "n"),
-    (0, 1): ("yxz", "g"),
-    (1, 0): ("myxz", "n"),
-    (1, 1): ("mzxy", "g"),
-    (2, 0): ("xyz", "n"),
-    (2, 1): ("xyz", "g"),
+    (0, 0): ("yxz", "nr"),
+    (0, 1): ("xyz", "gr"),
+    (1, 0): ("myxz", "nr"),
+    (1, 1): ("xyz", "gr"),
+    (2, 0): ("mzxy", "nr"),
+    (2, 1): ("xyz", "gr"),
 }
 PLAN = {
-    ("O", 0, 1): ((0, 0), (0, 1)),
-    ("M", 1, 1): ((0, 1), (1, 0)),
-    ("M", 2, 1): ((1, 1),),
-    ("O", 1): ((0, 1),),
-    ("O", 2, 0): ((1, 1), (1, 0), (2, 0), (0, 1), (0, 0), (1, 1)),
-    ("O", 2, 1): ((2, 0), (1, 0), (0, 1)),
-    ("rows",): ((1, 1),),
-    ("residual",): ((2, 1), (2, 0)),
-    ("outputs",): ("mixed", (2, 0)),
-    ("own", 0): ((0, 0), (2, 0), (2, 1), (0, 0), (1, 0)),
-    ("own", 1): ((1, 1), (0, 0)),
-    ("own", 2): ((1, 0), (2, 0)),
-    ("other", 1): ((1, 1), (0, 1), (1, 0), (0, 0), "small", (2, 0)),
-    ("token other",): ((2, 1), (1, 0), (1, 1), "small", (2, 1), (0, 1)),
-    ("norm",): ((0, 0), (1, 0), "small", (1, 1), (2, 1), (2, 1), (0, 1), (0, 0), (1, 1), "small", (1, 0), "small"),
-    ("end",): ((2, 1), (2, 0)),
+    ("O", 0, 1): ((0, 1), (0, 0)),
+    ("M", 2, 0): ((2, 0), (1, 0)),
+    ("O", 1): ((0, 0), (2, 0), (0, 0), (0, 1)),
+    ("O", 1, 1): ((1, 0),),
+    ("O", 2, 1): ((1, 1), (0, 0), (2, 0)),
+    ("rows",): ((0, 0), (0, 1)),
+    ("residual",): ((2, 0), (1, 0)),
+    ("outputs",): ((1, 0),),
+    ("own", 0): ((0, 0),),
+    ("own", 1): ((2, 0), (1, 1), (1, 0), (2, 1)),
+    ("own", 2): ((0, 0), (2, 0)),
+    ("other", 0): ((0, 1), (0, 0), (1, 1), (2, 0)),
+    ("other", 1): ((1, 0),),
+    ("token other",): (
+        (2, 1), (0, 1), "small", "mixed", (2, 0), (1, 1), (0, 1), (1, 0), (2, 1), "small", (1, 1), (2, 1),
+        (2, 0), (1, 1), (0, 1), "small", (0, 0),
+    ),
+    ("norm",): ((1, 0), (2, 1), "small", (2, 1), (2, 0), (1, 1)),
+    ("end",): ("small", (2, 1), (1, 0)),
 }
 
 
@@ -91,6 +94,7 @@
             self.ways, self.plan = WAYS, PLAN
         self.chan_first = [unit for unit in self.units if self.ways[unit][0] in ("yxz", "myxz")]
         self.dp_first = [unit for unit in self.units if self.ways[unit][0] in ("zxy", "mzxy")]
+        self.loads = 16
         self.plane = 2 * self.hid
         self.blocks = -(-self.f // self.l)
         self.vec_wide = max(self.f, self.l)
@@ -99,7 +103,7 @@
         self.small = pad_to(self.vec_row + 8 * groups, 64 * self.xs)
         self.groups = (self.small - self.vec_row) // 8
         self.piece = self.small // (4 * self.xs)
-        assert mesh_shape["chan"] == 2 and self.hid % 2 == 0 and self.images % 2 == 0 and self.images <= 8
+        assert self.own >= 3 and mesh_shape["chan"] == 2 and self.hid % 2 == 0 and self.images % 2 == 0 and self.images <= 8
         assert 1 << self.levels == self.dp and self.f % self.l == 0 and self.ds == self.l
 
 
@@ -121,7 +125,8 @@
     tin, th, tslope, msend, mrecv, rows_m, rows_n, inv2, vec_in = get(9)
     xs_all, gs_all, w_up, w_dn, w_b, hid_s, pg_s, out_own, ng_own, stage, ng_in, out_in = get(12)
     blow, gacc, vecs, small_send, small_c, small_p, small_in, small_z = get(8)
-    gm, gb, rx, yb, ry = get(P_), get(P_), get(P_), get(P_), get(P_)
+    (gm,) = get(1)
+    gb, rx, yb, ry = get(P_), get(P_), get(P_), get(P_)
     zb, rz = dict(zip(o.units, get(2 * P_))), dict(zip(o.units, get(2 * P_)))
     ryo = {unit: next(names) for unit in o.chan_first}
     rzo = {unit: next(names) for unit in o.dp_first}
@@ -184,7 +189,7 @@
     stores = []
 
     def store(src, dst):
-        copy = pltpu.make_async_copy(src, dst, loc_sem.at[24 + len(stores)])
+        copy = pltpu.make_async_copy(src, dst, loc_sem.at[o.loads + len(stores)])
         copy.start()
         stores.append(copy)
 
@@ -208,7 +213,6 @@
         rows_n[i, S:PS, :] = jnp.zeros((pad, o.d), F32)
         rows_m[i, S:PS, :] = jnp.zeros((pad, o.d), BF)
         inv2[i, S:PS, :] = jnp.zeros((pad, 1), F32)
-        msend[i, S:PS, :] = jnp.zeros((pad, L), BF)
     vecs[...] = jnp.zeros(vecs.shape, F32)
     gacc[...] = jnp.zeros(gacc.shape, F32)
     vec_ref[...] = jnp.zeros(vec_ref.shape, F32)
@@ -259,10 +263,13 @@
     copy_w = {}
     copy_f = {}
 
+    def weight_rows(part):
+        start, size = o.fetches[part]
+        return pl.ds(pl.multiple_of(start + bit * (size // 2), 16), size // 2)
+
     def weight_spans(step, part):
         start, size = o.fetches[part]
-        cols = pl.ds(start, size)
-        rows_dn = pl.ds(pl.multiple_of(start + bit * (size // 2), 16), size // 2)
+        cols, rows_dn = pl.ds(start, size), weight_rows(part)
         rows_own = pl.ds(start, size) if part else rows_dn
         return (
             (chan_up_ref.at[near_from, cols], w_up.at[step, near, cols], y),
@@ -274,6 +281,8 @@
         for step in range(1, X):
             for n in which if part < len(o.fetches) else ():
                 src, dst, yy = weight_spans(step, part)[n]
+                if part and n == 2:
+                    src, yy = w_dn.at[0, weight_rows(part), pl.ds(L, L)], y
                 copy_w[step, part, n] = send(src, dst, dev(xx=(x + step) % X, yy=yy))
 
     def hand_on(part, which):
@@ -286,6 +295,11 @@
                     copy_w[step, part, n].wait()
                     copy_f[step, part, n] = send(dst, dst, z_pair)
 
+    def want(group, which):
+        for step in range(1, X):
+            for n in which:
+                copy_f[step, group, n].wait()
+
     quarter = F // 4
     bit2 = (z // 2) % 2
     z_far = dev(zz=z + 2 - 4 * bit2)
@@ -303,8 +317,13 @@
         copy_dn2.append(send(ref, ref, peer))
 
     fetch(0, (0,))
-    copy_cot = send(cot_ref.at[pl.ds((1 - y) * OWN, OWN)], cot_in, partner)
+    cot_sems = take(OWN)
+
+    def copy_cot(i):
+        return remote(cot_ref.at[(1 - y) * OWN + i], cot_in.at[i], partner, cot_sems + i)
+
     fetch(0, (1, 2))
+    copy_cot(0).start()
 
     copy_stats.wait()
     total = (stats[0] + stats_in[0]) * (1.0 / width)
@@ -339,35 +358,20 @@
 
     @pl.loop(0, OWN)
     def _(i):
-        msend[i, :S, :] = token_forward((1 - y) * OWN + i).astype(BF)
+        msend[i] = token_forward((1 - y) * OWN + i).astype(BF)
         copy_mixed(i).start()
+
+    copy_cot(1).start()
+    dn2_on(dn2_mine, z_far)
+    hand_on(0, (0,))
 
     @pl.loop(0, OWN)
     def _(i):
         rows_n[i, :S, :L] = token_forward(y * OWN + i)
 
-    dn2_on(dn2_mine, z_far)
-    hand_on(0, (0,))
+    hand_on(0, (1, 2))
     fetch(1, (1,))
-    hand_on(0, (1, 2))
     dn2_on(dn2_half, z_pair)
-    load_cot.wait()
-    copy_cot.wait()
-    load_live.wait()
-    live = live_ref[0]
-
-    def keep_of(j):
-        return jnp.where(j < live, 1.0, 0.0).astype(F32)
-
-    @pl.loop(0, OWN)
-    def _(i):
-        keep = keep_of(y * OWN + i)
-        gs_all[c, i, :S, :L] = (cot[i].astype(F32) * keep).astype(BF)
-        gs_all[c, i, :S, L:] = (cot_in[i].astype(F32) * keep).astype(BF)
-
-    copy_gs = send(gs_all.at[c], gs_all.at[c], sibling)
-    hand_on(1, (0,))
-
     copy_vec.wait()
     both = [jnp.concatenate([vec_ref[n:n + 1, :L], vec_in[n:n + 1, :L]], axis=1) for n in range(2, 5)]
     second_gain, second_shift, down_bias = both
@@ -376,10 +380,9 @@
     def copy_rows(i):
         return remote(xs_all.at[c, i], xs_all.at[c, i], sibling, row_sems + i)
 
-    @pl.loop(0, OWN)
-    def _(i):
+    def second_norm(i):
         copy_mixed(i).wait()
-        rows_n[i, :S, L:] = mrecv[i, :S, :].astype(F32)
+        rows_n[i, :S, L:] = mrecv[i].astype(F32)
         v = rows_n[i, :S, :]
         mean = jnp.sum(v, -1, keepdims=True) * (1.0 / width)
         spread = jnp.sum(v * v, -1, keepdims=True) * (1.0 / width) - mean * mean
@@ -391,16 +394,105 @@
         xs_all[c, i, :S, :] = (normed * second_gain + second_shift).astype(BF)
         copy_rows(i).start()
 
-    fetch(1, (2,))
-    hand_on(1, (1,))
+    load_cot.wait()
+    load_live.wait()
+    live = live_ref[0]
+    gs_sems = take(OWN)
+
+    def keep_of(j):
+        return jnp.where(j < live, 1.0, 0.0).astype(F32)
+
+    def copy_gs(i):
+        return remote(gs_all.at[c, i], gs_all.at[c, i], sibling, gs_sems + i)
+
+    def out_grads(i):
+        copy_cot(i).wait()
+        keep = keep_of(y * OWN + i)
+        gs_all[c, i, :S, :L] = (cot[i].astype(F32) * keep).astype(BF)
+        gs_all[c, i, :S, L:] = (cot_in[i].astype(F32) * keep).astype(BF)
+        copy_gs(i).start()
+
+    rows = OWN * PS
+
+    def inner(step, start, size, i, sums):
+        cols, block = pl.ds(start, size), pl.ds(pl.multiple_of(i * PS, 16), PS)
+        pre = nn(xs_all[:, i].reshape(2 * PS, o.d), w_up[step, :, cols]) + w_b[step, 0:1, cols]
+        value, slope = gelu_pair(pre)
+        hid_s[step, :, block, cols] = value.astype(BF).reshape(2, PS, size)
+        grad = (nt(gs_all[:, i].reshape(2 * PS, o.d), w_dn[step, cols, :]) * slope).astype(BF)
+        pg_s[step, :, block, cols] = grad.reshape(2, PS, size)
+        return sums + jnp.sum(grad.astype(F32), 0, keepdims=True)
+
+    def bias_sums(step, start, size, sums):
+        group = 3 + ((x + X - step) % X * 2 + c) * o.blocks
+        for n in range(start, start + size, 128):
+            block, lanes = n // L, n % L
+            vecs[group + block, 0:1, lanes:lanes + 128] = sums[:, n - start:n - start + 128]
+
+    def own_hidden(cc, i):
+        block = pl.ds(pl.multiple_of(i * PS, 16), PS)
+        value, slope = gelu_pair(nn(xs_all[cc, i], w_up[0]) + w_b[0, 0:1, :])
+        hid_s[0, cc, block, :] = value.astype(BF)
+        for n in range(o.blocks):
+            first = ((cc * o.blocks + n) * OWN + i) * PS
+            gm[pl.ds(pl.multiple_of(first, 16), PS), :] = slope[:, n * L:(n + 1) * L]
+
+    def own_back(i, sums):
+        block = pl.ds(pl.multiple_of(i * PS, 16), PS)
+        grad = nt(gs_all[:, i].reshape(2 * PS, o.d), w_dn[0])
+        for cc in range(2):
+            slopes = []
+            for n in range(o.blocks):
+                first = ((cc * o.blocks + n) * OWN + i) * PS
+                slopes.append(gm[pl.ds(pl.multiple_of(first, 16), PS), :])
+            mine = (grad[cc * PS:(cc + 1) * PS] * jnp.concatenate(slopes, 1)).astype(BF)
+            pg_s[0, cc, block, :] = mine
+            sums = sums + jnp.sum(mine.astype(F32), 0, keepdims=True)
+        return sums
+
+    def own_forward(i):
+        own_hidden(c, i)
+        copy_rows(i).wait()
+        own_hidden(1 - c, i)
+
+    def other_slots_first(i):
+        for step in range(1, X):
+            sums_o[step] = inner(step, start0, size0, i, sums_o[step])
+
+    start0, size0 = o.fetches[0]
+    sums_o = [jnp.zeros((1, size0), F32)] * X
+    sums_m = jnp.zeros((1, F), F32)
     load_up0.wait()
     load_up1.wait()
     load_dn.wait()
-    copy_gs.wait()
-
-    @pl.loop(0, OWN)
-    def _(i):
-        copy_rows(i).wait()
+    second_norm(0)
+    copy_cot(2).start()
+    own_forward(0)
+    out_grads(0)
+    second_norm(1)
+    hand_on(1, (0, 1))
+    own_forward(1)
+    for i in range(2, OWN):
+        second_norm(i)
+        own_forward(i)
+    want(0, (0, 1, 2))
+    for step in range(1, X):
+        copy_b[step].wait()
+    copy_gs(0).wait()
+    other_slots_first(0)
+    out_grads(1)
+    copy_dn2[-1].wait()
+    fetch(1, (2,))
+    sums_m = own_back(0, sums_m)
+    copy_gs(1).wait()
+    other_slots_first(1)
+    for i in range(2, OWN):
+        out_grads(i)
+        sums_m = own_back(i - 1, sums_m)
+        copy_gs(i).wait()
+        other_slots_first(i)
+    for step in range(1, X):
+        bias_sums(step, start0, size0, sums_o[step])
 
     def levels():
         start, count, used = 0, N, 0
@@ -415,11 +507,24 @@
     def my_segment():
         return list(levels())[-1][0]
 
+    def gm_rows(part, kind, half, span):
+        start, size = o.parts[part]
+        seg = size // N
+        first = 4 * start + (2 * kind + half) * size
+        return pl.ds(pl.multiple_of(first + span.start * seg, 8), span.size * seg)
+
+    def gm_get(part, kind, half, span):
+        seg = o.parts[part][1] // N
+        return gm[gm_rows(part, kind, half, span), :].reshape(span.size, seg, L)
+
+    def gm_set(part, kind, half, span, value):
+        gm[gm_rows(part, kind, half, span), :] = value.reshape(-1, L)
+
     def add(part, kind, half, span, *terms):
-        mine = gm[part][kind, half, span]
+        mine = gm_get(part, kind, half, span)
         for term in terms:
             mine = mine + term.astype(F32)
-        gm[part][kind, half, span] = mine
+        gm_set(part, kind, half, span, mine)
 
     everything = pl.ds(0, N)
     low, high = pl.ds(0, N // 2), pl.ds(N // 2, N // 2)
@@ -435,7 +540,7 @@
             span = pl.ds(used, count)
             copies = []
             for half in range(halves):
-                out[half, span] = gm[part][kind, half, pl.ds(send_at, count)].astype(BF)
+                out[half, span] = gm_get(part, kind, half, pl.ds(send_at, count)).astype(BF)
                 copies.append(send(out.at[half, span], land.at[half, span], peer))
             yield
             for half in range(halves):
@@ -446,7 +551,7 @@
         own = pl.ds(my_segment(), 1)
         done = finals(part, kind)
         early = kind == 0 and o.ways[part, kind][1] == "g"
-        done[0][own] = gm[part][kind, 0, own].astype(BF)
+        done[0][own] = gm_get(part, kind, 0, own).astype(BF)
         if early:
             copy = send(done[0].at[own], done[1].at[own], partner)
             yield
@@ -469,7 +574,7 @@
         return [send(gb[part].at[n, kind], rx[part].at[n, kind], owner(n)) for n in range(X - 1)]
 
     def send_y(part, kind, span):
-        yb[part][kind, span] = gm[part][kind, 1, span].astype(BF)
+        yb[part][kind, span] = gm_get(part, kind, 1, span).astype(BF)
         return send(yb[part].at[kind, span], ry[part].at[kind, span], partner)
 
     def wait_all(copies):
@@ -608,25 +713,6 @@
         for name in o.plan.get(point, ()):
             step_of(name)
 
-    rows = OWN * PS
-
-    def inner(step, start, size):
-        cols = pl.ds(start, size)
-
-        def side(cc, sums):
-            pre = nn(xs_all[cc].reshape(rows, o.d), w_up[step, :, cols]) + w_b[step, 0:1, cols]
-            value, slope = gelu_pair(pre)
-            hid_s[step, cc, :, cols] = value.astype(BF)
-            grad = (nt(gs_all[cc].reshape(rows, o.d), w_dn[step, cols, :]) * slope).astype(BF)
-            pg_s[step, cc, :, cols] = grad
-            return sums + jnp.sum(grad.astype(F32), 0, keepdims=True)
-
-        sums = lax.fori_loop(0, 2, side, jnp.zeros((1, size), F32))
-        group = 3 + ((x + X - step) % X * 2 + c) * o.blocks
-        for n in range(start, start + size, 128):
-            block, lanes = n // L, n % L
-            vecs[group + block, 0:1, lanes:lanes + 128] = sums[:, n - start:n - start + 128]
-
     def weight_grad(step, part, kind):
         start, size = o.parts[part]
         cols = pl.ds(start, size)
@@ -638,28 +724,30 @@
             if step:
                 gb[part][step - 1, kind, half] = block.astype(BF)
             else:
-                gm[part][kind, half] = block
+                gm_set(part, kind, half, everything, block)
 
     def other_slots(group):
         start, size = o.fetches[group]
-        for step in range(1, X):
-            if group == 0:
-                copy_b[step].wait()
-            for n in range(3):
-                copy_f[step, group, n].wait()
-            inner(step, start, size)
+        if group:
+            want(group, (0, 1, 2))
+            for step in range(1, X):
+                sums = lax.fori_loop(
+                    0, OWN, lambda i, t, step=step: inner(step, start, size, i, t), jnp.zeros((1, size), F32)
+                )
+                bias_sums(step, start, size, sums)
         at("O", group)
         for part in range(P_):
             if start <= o.parts[part][0] < start + size:
                 for kind in range(2):
                     for step in range(1, X):
                         weight_grad(step, part, kind)
+                    if part + kind == 0:
+                        hand_on(1, (2,))
                     at("O", part, kind)
 
     other_slots(0)
-    hand_on(1, (2,))
-    copy_dn2[-1].wait()
-    inner(0, 0, F)
+    sums_m = own_back(OWN - 1, sums_m)
+    bias_sums(0, 0, F, sums_m)
     at("M")
     for part in range(P_):
         for kind in range(2):
@@ -704,9 +792,9 @@
         m1 = jnp.sum(q, -1, keepdims=True) * (1.0 / width)
         m2 = jnp.sum(q * normed, -1, keepdims=True) * (1.0 / width)
         res = (back + inv2[i] * (q - m1 - normed * m2)).astype(BF)
-        mrecv[i] = res[:, L:]
+        mrecv[i] = res[:S, L:]
         copy_res(i).start()
-        blow[y * OWN + i] = res[:, :L]
+        blow[y * OWN + i] = res[:S, :L]
         return sums
 
     zero = jnp.zeros((1, o.d), F32)
@@ -721,10 +809,7 @@
     at("outputs 0")
     out_own[...] = row_sums(1, c)
 
-    mixed_sems2 = take(OWN)
-
-    def copy_mo(i):
-        return remote(msend.at[i], mixed_out.at[y * OWN + i], partner, mixed_sems2 + i)
+    copy_mo = remote(msend, mixed_out.at[pl.ds(y * OWN, OWN)], partner)
 
     def output_rows():
         copy_out.wait()
@@ -734,11 +819,11 @@
             block = pl.ds(pl.multiple_of(i * PS, 16), PS)
             branch = out_own[block, :] + out_in[block, :].astype(F32) + down_bias
             result = (keep_of(y * OWN + i) * (rows_m[i].astype(F32) + branch)).astype(BF)
-            msend[i] = result[:, L:]
-            copy_mo(i).start()
-            xs_all[c, i, :, :L] = result[:, :L]
-
-        store(xs_all.at[c, :, :, pl.ds(0, L)], mixed_out.at[pl.ds(y * OWN, OWN)])
+            msend[i] = result[:S, L:]
+            cot[i] = result[:S, :L]
+
+        copy_mo.start()
+        store(cot, mixed_out.at[pl.ds(y * OWN, OWN)])
         yield
 
     pipes["mixed"] = output_rows()
@@ -752,9 +837,9 @@
     def token_backward(j, carry):
         table, sum_gain, sum_shift, sum_bias = carry
         low_grad = blow[j]
-        grad = (nn(dn_s[...], low_grad) * tslope[j].astype(F32)).astype(BF)
+        grad = (nn(dn_s[:, :S], low_grad) * tslope[j].astype(F32)).astype(BF)
         gacc[0] += nt(tin[j], grad)
-        gacc[1] += nt(low_grad, th[j])
+        gacc[1, :S, :] += nt(low_grad, th[j])
         sum_bias = sum_bias + nt(ones, low_grad)
         back = nn(up_s[...], grad)
         normed, _ = first_norm(j)
@@ -766,7 +851,7 @@
         table = note(table, j, jnp.sum(back, -1, keepdims=True), jnp.sum(back * normed, -1, keepdims=True))
         return table, sum_gain, sum_shift, sum_bias
 
-    carry = (jnp.zeros((S, 128), F32), jnp.zeros((1, L), F32), jnp.zeros((1, L), F32), jnp.zeros((16, PS), F32))
+    carry = (jnp.zeros((S, 128), F32), jnp.zeros((1, L), F32), jnp.zeros((1, L), F32), jnp.zeros((16, S), F32))
     for i in range(OWN):
         carry = token_backward(y * OWN + i, carry)
         at("own", i)
@@ -779,7 +864,7 @@
     table, sum_gain, sum_shift, sum_bias = carry
     stats[1] = across(table)
     copy_stats2 = send(stats.at[1], stats_in.at[1], partner)
-    vecs[0, 0:1, :PS] = sum_bias[0:1, :]
+    vecs[0, 0:1, :S] = sum_bias[0:1, :]
     vecs[1 + y, 0:1, :] = sum_gain
     vecs[1 + y, 1:2, :] = sum_shift
 
@@ -848,7 +933,7 @@
         normed, inv_one = first_norm(j)
         grad = ng_own[scaled(j)][:S]
         grad = grad - column(means2[:S, :], j) - normed * column(means2[:S, :], j + 8)
-        blow[j, :S, :] = (blow[j, :S, :].astype(F32) + inv_one * grad).astype(BF)
+        blow[j] = (blow[j].astype(F32) + inv_one * grad).astype(BF)
 
     store(blow, grad_out)
     at("norm")
@@ -857,10 +942,7 @@
         for name in list(pipes):
             step_of(name)
 
-    @pl.loop(0, OWN)
-    def _(i):
-        copy_mo(i).wait()
-
+    copy_mo.wait()
     for copy in stores:
         copy.wait()
 
@@ -869,12 +951,19 @@
     I, S, PS, L, OWN, D, X, N, F = o.images, o.s, o.ps, o.l, o.own, o.d, o.xs, o.dp, o.f
     any_spec = pl.BlockSpec(memory_space=pl.ANY)
     rows = OWN * PS
-    copies = 16 + 4 * OWN + (X - 1) * (1 + 6 * len(o.parts)) + 6 * X + N
-    copies += len(o.units) * ((X - 1) * (3 + 2 * o.levels) + 5 * o.levels + 8)
+    groups = len(o.fetches)
+    copies = 2 + 4 + 5 * OWN + (X - 1) * (1 + 3 * groups + 3 + 2 * (groups - 1)) + 3 + 4 * X + N - 1
+    for unit in o.units:
+        way, order = o.ways[unit]
+        early = unit[1] == 0 and order == "g"
+        copies += o.levels * (1 + early) + (unit[1] == 0) + 1 + o.levels
+        if way in ("zxy", "mzxy", "xzy"):
+            copies += o.levels
+        copies += (X - 1) * {"xyz": 1, "xzy": 1, "yxz": 2, "myxz": 2}.get(way, 2 * o.levels + 1)
     segs = [size // N for _, size in o.parts]
     outs = [
-        jax.ShapeDtypeStruct((I, PS, L), BF),
-        jax.ShapeDtypeStruct((I, PS, L), BF),
+        jax.ShapeDtypeStruct((I, S, L), BF),
+        jax.ShapeDtypeStruct((I, S, L), BF),
         jax.ShapeDtypeStruct((o.small, L), BF),
     ]
     outs += [jax.ShapeDtypeStruct((2, N, seg, L), BF) for seg in segs]
@@ -888,19 +977,19 @@
         ((o.wide, 128), F32), ((o.wide, 128), F32),
         ((PS, L), BF), ((L, PS), BF), ((L, PS), BF), ((PS, L), BF), ((PS, 128), F32),
         ((I, PS, L), BF), ((I, o.ds, L), BF), ((I, o.ds, L), BF),
-        ((OWN, PS, L), BF), ((OWN, PS, L), BF),
+        ((OWN, S, L), BF), ((OWN, S, L), BF),
         ((OWN, PS, D), BF), ((OWN, PS, D), F32), ((OWN, PS, 1), F32), ((8, o.vec_wide), F32),
         ((2, OWN, PS, D), BF), ((2, OWN, PS, D), BF),
         ((X, D, F), BF), ((X, F, D), BF), ((X, 8, o.vec_wide), F32),
         ((X, 2, rows, F), BF), ((X, 2, rows, F), BF),
         ((rows, D), F32), ((2, rows, L), F32), ((2, rows, D), BF),
         ((rows, D), BF), ((rows, D), BF),
-        ((I, PS, L), BF), ((2, PS, L), F32), ((o.groups, 8, L), F32),
+        ((I, S, L), BF), ((2, PS, L), F32), ((o.groups, 8, L), F32),
         ((o.small, L), F32), ((o.small // 2, L), F32), ((o.small // 2, L), BF),
         ((2 * X - 1, o.piece, L), BF), ((N, o.piece, L), BF),
     ]
     blocks = [(N, seg, L) for seg in segs]
-    scratch += [((2, 2) + block, F32) for block in blocks]
+    scratch += [((4 * F, L), F32)]
     scratch += [((X - 1, 2, 2) + block, BF) for block in blocks] * 2
     scratch += [((2,) + block, BF) for block in blocks] * 2
     for _ in range(2):
@@ -915,7 +1004,7 @@
         in_specs=[any_spec] * (len(matrices) + len(vectors)),
         out_specs=[any_spec] * len(outs),
         scratch_shapes=[pltpu.VMEM(*entry) if entry else pltpu.SMEM((1,), jnp.int32) for entry in scratch]
-        + [pltpu.SemaphoreType.DMA((40,)), pltpu.SemaphoreType.DMA((copies,)), pltpu.SemaphoreType.DMA((copies,))],
+        + [pltpu.SemaphoreType.DMA((o.loads + 3 + len(o.units),)), pltpu.SemaphoreType.DMA((copies,)), pltpu.SemaphoreType.DMA((copies,))],
         compiler_params=pltpu.CompilerParams(
             collective_id=1, has_side_effects=True, vmem_limit_bytes=63 * 2**20
         ),
@@ -931,19 +1020,19 @@
         return [next(names) for _ in range(count)]
 
     inputs, outputs = get(3 + 2 * P_), get(14)
-    inputs_v, outputs_v = get(3 + 2 * P_), get(14)
+    inputs_v, outputs_v = get(3 + 2 * P_), get(12)
     in_sem, out_sem = get(2)
     S, PS, L = o.s, o.ps, o.l
     y = lax.axis_index("chan")
     h = lax.axis_index("hid")
     loads = [pltpu.make_async_copy(src, dst, in_sem.at[n]) for n, (src, dst) in enumerate(zip(inputs, inputs_v))]
+    outputs_v = inputs_v[:2] + outputs_v
     stores = [pltpu.make_async_copy(src, dst, out_sem.at[n]) for n, (src, dst) in enumerate(zip(outputs_v, outputs))]
-    order = list(range(3, 3 + 2 * P_)) + [0, 1, 2]
-    for n in order:
-        loads[n].start()
-    mixed_in, grad_in, small_in = inputs_v[:3]
+    for load in loads[3:] + loads[:3]:
+        load.start()
+    small_in = inputs_v[2]
     fin_up, fin_dn = inputs_v[3:3 + P_], inputs_v[3 + P_:]
-    mixed, grad, fg, fs, tu, tub, td, tdb, sg, ss, cu, cub, cd, cdb = outputs_v
+    _, _, fg, fs, tu, tub, td, tdb, sg, ss, cu, cub, cd, cdb = outputs_v
     for part, (start, size) in enumerate(o.parts):
         loads[3 + part].wait()
         for half in range(2):
@@ -954,12 +1043,9 @@
         loads[3 + P_ + part].wait()
         cd[start:start + size, :] = fin_dn[part][...].astype(F32).reshape(size, L)
     stores[12].start()
-    loads[0].wait()
-    mixed[...] = mixed_in[:, :S]
-    stores[0].start()
-    loads[1].wait()
-    grad[...] = grad_in[:, :S]
-    stores[1].start()
+    for n in range(2):
+        loads[n].wait()
+        stores[n].start()
     loads[2].wait()
     small = small_in[...].astype(F32)
     tu[...] = small[:S]
@@ -1018,7 +1104,7 @@
         in_specs=[any_spec] * len(results),
         out_specs=[any_spec] * len(shapes),
         scratch_shapes=[pltpu.VMEM(result.shape, BF) for result in results]
-        + [pltpu.VMEM(shape, kind) for shape, kind in shapes]
+        + [pltpu.VMEM(shape, kind) for shape, kind in shapes[2:]]
         + [pltpu.SemaphoreType.DMA((len(results),)), pltpu.SemaphoreType.DMA((len(shapes),))],
         compiler_params=pltpu.CompilerParams(vmem_limit_bytes=63 * 2**20),
         name="unpack",

time: 126 us -> 118 us (0.937)
  Pallas kernels: 125 us -> 117 us
    pallas_call x1, Pallas kernels: 120 us -> 112 us  [block_call(): pl.pallas_call(functools.partial(kernel, o), out_shape=outs, in_specs=[an...]
where the time goes in v4:
time: 118 us
  Pallas kernels  117 us (99%)
  between operations  1.46 us (1%)
    pallas_call x1, Pallas kernels, block_call(): pl.pallas_call(functools.partial(kernel, o), out_shape=outs, in_specs=[an...  112 us
    pallas_call x1, Pallas kernels, body(): pl.pallas_call(functools.partial(unpack, o), out_shape=[jax.ShapeDtypeStr...  4.3 us

profile of v4, /device:TPU:0, one launch (start us, length us, event | category | flops | bytes accessed | tf_op | source)
XLA Modules:
  0.0 118.2 jit_solution(8319170124913787951)
XLA Ops:
  1.3 112.5 %mixer_block.1 = (bf16[6,196,384]{2,1,0:T(8,128)(2,1)}, bf16[6,196,384]{2,1,0:T(8,128)(2,1)}, bf16[512,384]{1,0:T(8,128)(2,1)}, bf16[2,4,64,384]{3,2,1,0:T(8,128...) custom-call(s32[1]{0:T(128)S(6)} %copy.29.refs_0_, ...), custom_call_target="tpu_custom_call" | custom-call | tf_op jit(solution)/shard_map/mixer_block/pallas_call | solution.py:1001
  113.8 4.3 %unpack.1 = (bf16[6,196,384]{2,1,0:T(8,128)(2,1)}, bf16[6,196,384]{2,1,0:T(8,128)(2,1)}, f32[384]{0:T(512)}, f32[384]{0:T(512)}, f32[196,384]{1,0:T(8,128)}, /*i...) custom-call(bf16[6,196,384]{2,1,0:T(8,128)(2,1)} %get-tuple-element., ...), custom_call_target="tpu_custom_call" | custom-call | tf_op jit(solution)/shard_map/unpack/pallas_call | solution.py:1101

commit v5 on v4

--- a/solution.py
+++ b/solution.py
@@ -49,25 +49,25 @@
     (2, 1): ("xyz", "gr"),
 }
 PLAN = {
-    ("O", 0, 1): ((0, 1), (0, 0)),
-    ("M", 2, 0): ((2, 0), (1, 0)),
-    ("O", 1): ((0, 0), (2, 0), (0, 0), (0, 1)),
-    ("O", 1, 1): ((1, 0),),
-    ("O", 2, 1): ((1, 1), (0, 0), (2, 0)),
-    ("rows",): ((0, 0), (0, 1)),
-    ("residual",): ((2, 0), (1, 0)),
-    ("outputs",): ((1, 0),),
-    ("own", 0): ((0, 0),),
-    ("own", 1): ((2, 0), (1, 1), (1, 0), (2, 1)),
-    ("own", 2): ((0, 0), (2, 0)),
-    ("other", 0): ((0, 1), (0, 0), (1, 1), (2, 0)),
-    ("other", 1): ((1, 0),),
+    ("O", 0, 0): ((0, 0),),
+    ("M", 0, 0): ((0, 1),),
+    ("M", 1, 1): ((1, 0),),
+    ("M", 2, 0): ((2, 0),),
+    ("M", 2, 1): ((0, 0), (0, 0)),
+    ("O", 1): ((2, 0),),
+    ("O", 1, 1): ((0, 1),),
+    ("O", 2, 1): ((2, 0), (1, 1), (0, 0), (1, 0)),
+    ("rows",): ((2, 0),),
+    ("residual",): ((1, 0), (0, 0)),
+    ("outputs 0",): ((0, 1),),
+    ("outputs",): ((0, 0), (2, 0)),
+    ("own", 0): ((1, 0), (1, 1), (2, 1), (0, 0)),
+    ("own", 2): ((2, 0), (1, 0), (0, 0), (0, 1), (1, 0), (1, 1), (2, 0)),
     ("token other",): (
-        (2, 1), (0, 1), "small", "mixed", (2, 0), (1, 1), (0, 1), (1, 0), (2, 1), "small", (1, 1), (2, 1),
-        (2, 0), (1, 1), (0, 1), "small", (0, 0),
+        (2, 1), (1, 0), (1, 1), "small", "mixed", (2, 1), "small", (2, 0), (1, 1), (0, 1), (2, 1), "small",
+        (0, 0), (1, 1), (1, 0), (2, 1),
     ),
-    ("norm",): ((1, 0), (2, 1), "small", (2, 1), (2, 0), (1, 1)),
-    ("end",): ("small", (2, 1), (1, 0)),
+    ("norm",): ("small", (2, 0), (0, 1), (2, 1), (1, 0), (1, 1), (0, 1), "small", (2, 1), (2, 0)),
 }
 
 

time: 118 us -> 116 us (0.983)
  Pallas kernels: 117 us -> 115 us
    pallas_call x1, Pallas kernels: 112 us -> 111 us  [block_call(): pl.pallas_call(functools.partial(kernel, o), out_shape=outs, in_specs=[an...]
where the time goes in v5:
time: 116 us
  Pallas kernels  115 us (99%)
  between operations  1.46 us (1%)
    pallas_call x1, Pallas kernels, block_call(): pl.pallas_call(functools.partial(kernel, o), out_shape=outs, in_specs=[an...  111 us
    pallas_call x1, Pallas kernels, body(): pl.pallas_call(functools.partial(unpack, o), out_shape=[jax.ShapeDtypeStr...  4.3 us

profile of v5, /device:TPU:0, one launch (start us, length us, event | category | flops | bytes accessed | tf_op | source)
XLA Modules:
  0.0 116.3 jit_solution(9889991443309269556)
XLA Ops:
  1.3 110.5 %mixer_block.1 = (bf16[6,196,384]{2,1,0:T(8,128)(2,1)}, bf16[6,196,384]{2,1,0:T(8,128)(2,1)}, bf16[512,384]{1,0:T(8,128)(2,1)}, bf16[2,4,64,384]{3,2,1,0:T(8,128...) custom-call(s32[1]{0:T(128)S(6)} %copy.29.refs_0_, ...), custom_call_target="tpu_custom_call" | custom-call | tf_op jit(solution)/shard_map/mixer_block/pallas_call | solution.py:1001
  111.8 4.3 %unpack.1 = (bf16[6,196,384]{2,1,0:T(8,128)(2,1)}, bf16[6,196,384]{2,1,0:T(8,128)(2,1)}, f32[384]{0:T(512)}, f32[384]{0:T(512)}, f32[196,384]{1,0:T(8,128)}, /*i...) custom-call(bf16[6,196,384]{2,1,0:T(8,128)(2,1)} %get-tuple-element., ...), custom_call_target="tpu_custom_call" | custom-call | tf_op jit(solution)/shard_map/unpack/pallas_call | solution.py:1101

commit v6 on v4

--- a/solution.py
+++ b/solution.py
@@ -41,33 +41,32 @@
 
 
 WAYS = {
-    (0, 0): ("yxz", "nr"),
-    (0, 1): ("xyz", "gr"),
-    (1, 0): ("myxz", "nr"),
-    (1, 1): ("xyz", "gr"),
-    (2, 0): ("mzxy", "nr"),
-    (2, 1): ("xyz", "gr"),
+    (0, 0): ("yxz", "g"),
+    (0, 1): ("xyz", "g"),
+    (1, 0): ("myxz", "n"),
+    (1, 1): ("xyz", "g"),
+    (2, 0): ("mzxy", "n"),
+    (2, 1): ("xyz", "g"),
 }
 PLAN = {
-    ("O", 0, 1): ((0, 1), (0, 0)),
+    ("O", 0, 1): ((0, 0), (0, 1)),
     ("M", 2, 0): ((2, 0), (1, 0)),
-    ("O", 1): ((0, 0), (2, 0), (0, 0), (0, 1)),
-    ("O", 1, 1): ((1, 0),),
-    ("O", 2, 1): ((1, 1), (0, 0), (2, 0)),
-    ("rows",): ((0, 0), (0, 1)),
-    ("residual",): ((2, 0), (1, 0)),
-    ("outputs",): ((1, 0),),
-    ("own", 0): ((0, 0),),
-    ("own", 1): ((2, 0), (1, 1), (1, 0), (2, 1)),
-    ("own", 2): ((0, 0), (2, 0)),
-    ("other", 0): ((0, 1), (0, 0), (1, 1), (2, 0)),
-    ("other", 1): ((1, 0),),
+    ("O", 1): ((0, 0), (0, 0), (2, 0)),
+    ("O", 1, 0): ((0, 1),),
+    ("O", 2, 1): ((1, 1), (2, 0), (0, 0), (1, 0)),
+    ("rows",): ((0, 1), (2, 0)),
+    ("residual",): ((1, 0),),
+    ("outputs 0",): ((0, 0), (2, 1), (0, 1)),
+    ("outputs",): ((1, 0), (2, 0), (0, 0), (1, 1)),
+    ("own", 0): ((0, 1), (0, 0), (0, 1)),
+    ("own", 2): ((1, 0), (2, 1)),
+    ("other", 0): ((1, 1),),
     ("token other",): (
-        (2, 1), (0, 1), "small", "mixed", (2, 0), (1, 1), (0, 1), (1, 0), (2, 1), "small", (1, 1), (2, 1),
-        (2, 0), (1, 1), (0, 1), "small", (0, 0),
+        (1, 0), (2, 0), "small", (2, 1), (1, 1), "mixed", (2, 0), (1, 0), (2, 1), "small", (1, 1), (2, 1),
+        (1, 0), (2, 0), (0, 0),
     ),
-    ("norm",): ((1, 0), (2, 1), "small", (2, 1), (2, 0), (1, 1)),
-    ("end",): ("small", (2, 1), (1, 0)),
+    ("norm",): ("small", (2, 1), (1, 1), (0, 1), (2, 0), (2, 1), "small", (2, 0), (1, 0)),
+    ("end",): ("small", (0, 0), (1, 1)),
 }
 
 

time: 118 us -> 116 us (0.983)
  Pallas kernels: 117 us -> 114 us
    pallas_call x1, Pallas kernels: 112 us -> 110 us  [block_call(): pl.pallas_call(functools.partial(kernel, o), out_shape=outs, in_specs=[an...]
where the time goes in v6:
time: 116 us; the launch traced here: 115 us
  Pallas kernels  114 us (98%)
  between operations  1.48 us (1%)
    pallas_call x1, Pallas kernels, block_call(): pl.pallas_call(functools.partial(kernel, o), out_shape=outs, in_specs=[an...  110 us
    pallas_call x1, Pallas kernels, body(): pl.pallas_call(functools.partial(unpack, o), out_shape=[jax.ShapeDtypeStr...  4.3 us

profile of v6, /device:TPU:0, one launch (start us, length us, event | category | flops | bytes accessed | tf_op | source)
XLA Modules:
  0.0 115.4 jit_solution(10382371178900864468)
XLA Ops:
  1.3 109.6 %mixer_block.1 = (bf16[6,196,384]{2,1,0:T(8,128)(2,1)}, bf16[6,196,384]{2,1,0:T(8,128)(2,1)}, bf16[512,384]{1,0:T(8,128)(2,1)}, bf16[2,4,64,384]{3,2,1,0:T(8,128...) custom-call(s32[1]{0:T(128)S(6)} %copy.29.refs_0_, ...), custom_call_target="tpu_custom_call" | custom-call | tf_op jit(solution)/shard_map/mixer_block/pallas_call | solution.py:1000
  110.9 4.3 %unpack.1 = (bf16[6,196,384]{2,1,0:T(8,128)(2,1)}, bf16[6,196,384]{2,1,0:T(8,128)(2,1)}, f32[384]{0:T(512)}, f32[384]{0:T(512)}, f32[196,384]{1,0:T(8,128)}, /*i...) custom-call(bf16[6,196,384]{2,1,0:T(8,128)(2,1)} %get-tuple-element., ...), custom_call_target="tpu_custom_call" | custom-call | tf_op jit(solution)/shard_map/unpack/pallas_call | solution.py:1100
